TPU v7x, 32 devices: a whole 2x2x4 slice. The times are simulated.
32 devices in a mesh: gx: 4 (over z), gy: 8 (over y, x, core).
Axes of the slice: x: 2, y: 2, z: 4, core: 2. Of those that a mesh axis runs over, the one named last changes fastest.
Arguments:
- counts: int32 [32], replicated, may hold values from 1 to 12, as said below
- probes: bfloat16 [96, 4, 128, 512], P(None, 'gx', None, 'gy'), may hold values from -6 to 6
- blocks: bfloat16 [4, 8, 12, 24, 128, 128], P('gx', 'gy'), may hold values from -0.0546875 to 0.0546875
- pattern: int32 [4, 8, 12, 24], P('gx', 'gy'), may hold values from 0 to 107, as said below
- coeffs: float32 [4], replicated, may hold values from 0.2 to 1
Outputs:
- applied: float32 [4, 8, 12, 128, 512], P('gx', 'gy')
Inputs may be any that keep to these rules, and one draw needn't show every extreme that they name: `counts`: some domain holds exactly 12 panels in every draw. `pattern`: every entry names a live panel of its neighbourhood (below that domain's count). Slots 0 to 7 have code 4 (the own domain), slot 0 the panel itself taken modulo the own count; the other slots have codes other than 4.
All inputs are finite; a program needn't handle non-finite values.
Results may differ from a plain program's by a relative error of at most 0.0047.
Values may be sent and summed in bfloat16 or wider, within the bound.
A program may use at most 192 MiB of HBM per device.

v0:
```python
import jax
import jax.numpy as jnp
from jax import lax
from jax.sharding import PartitionSpec as P

STEPS = 3


def extended(cells, sides, width):
    for axis, dim in sides:
        count = lax.axis_size(axis)
        head = lax.slice_in_dim(cells, 0, width, axis=dim)
        tail = lax.slice_in_dim(cells, cells.shape[dim] - width, cells.shape[dim], axis=dim)
        cells = jnp.concatenate(
            [
                lax.ppermute(tail, axis, [(i, (i + 1) % count) for i in range(count)]),
                cells,
                lax.ppermute(head, axis, [((i + 1) % count, i) for i in range(count)]),
            ],
            axis=dim,
        )
    return cells


def gather_halo(block_state, capacity, panel_rows, probe_cols):
    padded = extended(block_state[None, None], (("gx", 0), ("gy", 1)), 1)
    return padded.reshape(9 * capacity, panel_rows, probe_cols)


def local(counts, probes, blocks, pattern, coeffs):
    grid_rows = lax.axis_size("gx")
    grid_cols = lax.axis_size("gy")
    capacity = blocks.shape[2]
    panel_rows = blocks.shape[4]
    part_cols = probes.shape[3]
    probe_cols = part_cols * grid_cols
    per_peer = (capacity + grid_rows - 1) // grid_rows
    my_row = lax.axis_index("gx")
    my_domain = my_row * grid_cols + lax.axis_index("gy")
    offsets = jnp.cumsum(counts) - counts
    first_row = (my_row - offsets) % grid_rows
    local_rows = first_row[:, None] + grid_rows * jnp.arange(per_peer, dtype=jnp.int32)[None, :]
    is_sent = local_rows < counts[:, None]
    source_slots = jnp.where(is_sent, (offsets[:, None] + local_rows) // grid_rows, 0)
    held_panels = probes[:, 0]
    outgoing = jnp.where(
        is_sent[:, :, None, None], held_panels[source_slots], jnp.zeros((), held_panels.dtype)
    )
    my_count = counts[my_domain]
    my_offset = offsets[my_domain]
    panels = jnp.arange(capacity, dtype=jnp.int32)
    owner_row = (my_offset + panels) % grid_rows
    peer_slot = panels // grid_rows
    arrived = lax.all_to_all(outgoing, ("gx", "gy"), split_axis=0, concat_axis=3, tiled=True)
    arrived = arrived.reshape(per_peer, panel_rows, grid_rows, probe_cols)
    picked = arrived[peer_slot, :, owner_row, :]
    is_live = panels < my_count
    start_panels = jnp.where(is_live[:, None, None], picked, jnp.zeros((), picked.dtype))
    live_mask = is_live.astype(jnp.float32)[:, None, None]
    halo_index = pattern[0, 0]
    local_blocks = blocks[0, 0]

    def operate(block_state):
        flat_halo = gather_halo(block_state, capacity, panel_rows, probe_cols)
        all_pieces = flat_halo[halo_index]
        summed = jnp.einsum(
            "rkab,rkbw->raw", local_blocks, all_pieces, preferred_element_type=jnp.float32
        )
        return summed * live_mask

    previous = start_panels.astype(jnp.float32)
    current = operate(start_panels)
    result = coeffs[0] * previous + coeffs[1] * current
    for degree in range(2, STEPS + 1):
        sent_panels = current.astype(jnp.bfloat16)
        following = 2.0 * operate(sent_panels) - previous
        result = result + coeffs[degree] * following
        previous, current = (current, following)
    return result[None, None]


def solution(mesh):
    in_specs = (
        P(),
        P(None, "gx", None, "gy"),
        P("gx", "gy", None, None, None, None),
        P("gx", "gy", None, None),
        P(),
    )
    out_specs = P("gx", "gy", None, None, None)
    return jax.shard_map(local, mesh=mesh, in_specs=in_specs, out_specs=out_specs, check_vma=False)
```

profile of v0, /device:TPU:1, one launch (start us, length us, event | category | flops | bytes accessed | tf_op | source)
XLA Modules:
  0.0 740.2 jit_solution(5116210494960575283)
XLA Ops:
  5.6 7.1 all-to-all-start
  15.4 34.4 %all-to-all-done = bf16[32,3,128,64]{2,3,1,0:T(8,128)(2,1)S(1)} async-done(((bf16[32,3,128,64]{2,3,1,0:T(8,128)(2,1)}), bf16[32,3,128,64]{2,3,1,0:T(8,128)(2,1)S(1)}, u32[]{:S(2)}, u32[]{:S(2)}) %all-to-all-start) | async-done | bytes 1572896 | tf_op jit(solution)/shard_map/all_to_all | solution.py:54
  52.2 2.7 collective-permute-start.1
  54.9 33.7 %collective-permute-done = bf16[1,1,12,128,512]{4,3,2,1,0:T(8,128)(2,1)S(1)} collective-permute-done((bf16[1,1,12,128,512]{4,3,2,1,0:T(8,128)(2,1)S(1)}, bf16[1,1,12,128,512]{4,3,2,1,0:T(8,128)(2,1)S(1)}, u32[]{:S(2)}, u32[]{:S(2)}) %collective-permute-start) | collective-permute-done | bytes 1572896 | tf_op jit(solution)/shard_map/ppermute | solution.py:16
  88.5 32.9 %collective-permute-done.1 = bf16[1,1,12,128,512]{4,3,2,1,0:T(8,128)(2,1)S(1)} collective-permute-done((bf16[1,1,12,128,512]{4,3,2,1,0:T(8,128)(2,1)S(1)}, bf16[1,1,12,128,512]{4,3,2,1,0:T(8,128)(2,1)S(1)}, u32[]{:S(2)}, u32[]{:S(2)}) %collective-permute-start.1) | collective-permute-done | bytes 1572896 | tf_op jit(solution)/shard_map/ppermute | solution.py:18
  127.3 99.3 %collective-permute-done.2 = bf16[3,1,12,128,512]{4,3,2,1,0:T(8,128)(2,1)} collective-permute-done((bf16[3,1,12,128,512]{4,3,2,1,0:T(8,128)(2,1)}, bf16[3,1,12,128,512]{4,3,2,1,0:T(8,128)(2,1)}, u32[]{:S(2)}, u32[]{:S(2)}) %collective-permute-start.2) | collective-permute-done | bytes 4718624 | tf_op jit(solution)/shard_map/ppermute | solution.py:16
  229.3 10.2 %pad_maximum_fusion = bf16[3,3,12,128,512]{4,3,2,1,0:T(8,128)(2,1)} fusion(bf16[3,1,12,128,512]{4,3,2,1,0:T(8,128)(2,1)} %collective-permute-done.3, bf16[1,1,12,128,512]{4,3,2,1,0:T(8,128)(2,1)} %copy-done.4, bf16[1,1,12,128,512]{4,3,2,1,0:T(8,128)(2,1)S(1)} %bitcast_select_fusion, bf16[1,1,12,128,512]{4,3,2,1,0:T(8,128)(2,1)} %copy-done.3, ...), kind=kLoop, calls=%fused_computation.5 | loop fusion | flops 28311552 | bytes 28311552 | tf_op jit(solution)/shard_map/concatenate | solution.py:14
  239.5 20.4 %gather_fusion.2 = bf16[288,128,512]{2,1,0:T(8,128)(2,1)} fusion(bf16[108,128,512]{2,1,0:T(8,128)(2,1)} %bitcast.85, s32[1024]{0:T(1024)S(1)} %pad_clamp_fusion), kind=kCustom, calls=%fused_computation.2 | custom fusion | bytes 75498624 | tf_op jit(solution)/shard_map/gather | solution.py:65
  259.9 19.1 %fusion.4 = f32[12,512,128,1]{2,1,3,0:T(8,128)S(1)} fusion(bf16[12,24,128,512]{3,2,1,0:T(8,128)(2,1)} %bitcast.87, bf16[1,1,12,24,128,128]{5,4,3,2,1,0:T(8,128)(2,1)} %param.7), kind=kOutput, calls=%fused_computation.12 | convolution fusion | flops 4831838208 | bytes 50331648 | tf_op jit(solution)/shard_map/rkab,rkbw->raw/dot_general | solution.py:66
  282.8 34.2 %collective-permute-done.4 = bf16[1,1,12,128,512]{3,4,2,1,0:T(8,128)(2,1)S(1)} collective-permute-done((bf16[1,1,12,128,512]{3,4,2,1,0:T(8,128)(2,1)S(1)}, bf16[1,1,12,128,512]{3,4,2,1,0:T(8,128)(2,1)S(1)}, u32[]{:S(2)}, u32[]{:S(2)}) %collective-permute-start.4) | collective-permute-done | bytes 1572896 | tf_op jit(solution)/shard_map/ppermute | solution.py:16
  317.0 32.5 %collective-permute-done.5 = bf16[1,1,12,128,512]{3,4,2,1,0:T(8,128)(2,1)S(1)} collective-permute-done((bf16[1,1,12,128,512]{3,4,2,1,0:T(8,128)(2,1)S(1)}, bf16[1,1,12,128,512]{3,4,2,1,0:T(8,128)(2,1)S(1)}, u32[]{:S(2)}, u32[]{:S(2)}) %collective-permute-start.5) | collective-permute-done | bytes 1572896 | tf_op jit(solution)/shard_map/ppermute | solution.py:18
  355.4 96.1 %collective-permute-done.6 = bf16[3,1,12,128,512]{3,4,2,1,0:T(8,128)(2,1)} collective-permute-done((bf16[3,1,12,128,512]{3,4,2,1,0:T(8,128)(2,1)}, bf16[3,1,12,128,512]{3,4,2,1,0:T(8,128)(2,1)}, u32[]{:S(2)}, u32[]{:S(2)}) %collective-permute-start.6) | collective-permute-done | bytes 4718624 | tf_op jit(solution)/shard_map/ppermute | solution.py:16
  451.5 5.5 collective-permute-done.7
  457.0 10.2 %pad_maximum_fusion.1 = bf16[3,3,12,128,512]{3,4,2,1,0:T(8,128)(2,1)} fusion(bf16[3,1,12,128,512]{3,4,2,1,0:T(8,128)(2,1)} %collective-permute-done.7, bf16[1,1,12,128,512]{3,4,2,1,0:T(8,128)(2,1)} %copy-done.6, bf16[1,1,12,128,512]{3,4,2,1,0:T(8,128)(2,1)S(1)} %fusion.19, bf16[1,1,12,128,512]{3,4,2,1,0:T(8,128)(2,1)} %copy-done.5, ...), kind=kLoop, calls=%fused_computation.6 | loop fusion | flops 28311552 | bytes 28311552 | tf_op jit(solution)/shard_map/concatenate | solution.py:14
  467.2 20.5 %gather_fusion.3 = bf16[288,128,512]{1,2,0:T(8,128)(2,1)} fusion(bf16[108,128,512]{1,2,0:T(8,128)(2,1)} %bitcast.86, s32[1024]{0:T(1024)S(1)} %pad_clamp_fusion), kind=kCustom, calls=%fused_computation.3 | custom fusion | bytes 75498624 | tf_op jit(solution)/shard_map/gather | solution.py:65
  487.8 20.3 %convert_subtract_fusion = f32[12,128,512]{1,2,0:T(8,128)} fusion(bf16[12,24,128,512]{2,3,1,0:T(8,128)(2,1)} %bitcast.89, bf16[1,1,12,24,128,128]{5,4,3,2,1,0:T(8,128)(2,1)} %param.7, f32[12]{0:T(128)S(1)} %fusion.37, bf16[12,128,512]{1,2,0:T(8,128)(2,1)S(1)} %copy-done.7, pred[12]{0:T(512)(128)(4,1)S(1)} %iota_compare_fusion), kind=kOutput, calls=%fused_computation.17 | convolution fusion | flops 4835770368 | bytes 51904572 | tf_op jit(solution)/shard_map/rkab,rkbw->raw/dot_general | solution.py:66
  513.6 33.2 %collective-permute-done.8 = bf16[1,1,12,128,512]{3,4,2,1,0:T(8,128)(2,1)S(1)} collective-permute-done((bf16[1,1,12,128,512]{3,4,2,1,0:T(8,128)(2,1)S(1)}, bf16[1,1,12,128,512]{3,4,2,1,0:T(8,128)(2,1)S(1)}, u32[]{:S(2)}, u32[]{:S(2)}) %collective-permute-start.8) | collective-permute-done | bytes 1572896 | tf_op jit(solution)/shard_map/ppermute | solution.py:16
  546.8 35.3 %collective-permute-done.9 = bf16[1,1,12,128,512]{3,4,2,1,0:T(8,128)(2,1)S(1)} collective-permute-done((bf16[1,1,12,128,512]{3,4,2,1,0:T(8,128)(2,1)S(1)}, bf16[1,1,12,128,512]{3,4,2,1,0:T(8,128)(2,1)S(1)}, u32[]{:S(2)}, u32[]{:S(2)}) %collective-permute-start.9) | collective-permute-done | bytes 1572896 | tf_op jit(solution)/shard_map/ppermute | solution.py:18
  583.9 98.0 %collective-permute-done.10 = bf16[3,1,12,128,512]{3,4,2,1,0:T(8,128)(2,1)S(1)} collective-permute-done((bf16[3,1,12,128,512]{3,4,2,1,0:T(8,128)(2,1)S(1)}, bf16[3,1,12,128,512]{3,4,2,1,0:T(8,128)(2,1)S(1)}, u32[]{:S(2)}, u32[]{:S(2)}) %collective-permute-start.10) | collective-permute-done | bytes 4718624 | tf_op jit(solution)/shard_map/ppermute | solution.py:16
  681.9 5.5 collective-permute-done.11
  687.4 5.2 pad_maximum_fusion.2
  692.6 20.4 %gather_fusion.4 = bf16[288,128,512]{1,2,0:T(8,128)(2,1)} fusion(bf16[108,128,512]{1,2,0:T(8,128)(2,1)} %bitcast.84, s32[1024]{0:T(1024)S(1)} %pad_clamp_fusion), kind=kCustom, calls=%fused_computation.4 | custom fusion | bytes 75498624 | tf_op jit(solution)/shard_map/gather | solution.py:65
  713.0 23.7 %fusion.9 = f32[1,1,12,128,512]{3,4,2,1,0:T(8,128)} fusion(f32[12,128,512]{1,2,0:T(8,128)} %convert_subtract_fusion, f32[12,512,128,1]{2,1,3,0:T(8,128)} %copy-done.2, bf16[12,24,128,512]{2,3,1,0:T(8,128)(2,1)} %bitcast.88, bf16[1,1,12,24,128,128]{5,4,3,2,1,0:T(8,128)(2,1)} %param.7, f32[]{:T(128)} %bitcast.28, f32[]{:T(128)} %bitcast.19, ...), kind=kOutput, calls=%fused_computation.22 | convolution fusion | flops 4842061824 | bytes 58196044 | tf_op jit(solution)/shard_map/rkab,rkbw->raw/dot_general | solution.py:66
  736.7 3.5 copy.25
  (65 shorter events, 35.9 us)
Async XLA Ops:
  0.0 3.4 copy-start
  4.3 9.1 %copy-start.8 = (s32[32]{0:T(128)S(1)}, s32[32]{0:T(128)}, u32[]{:S(2)}) copy-start(s32[32]{0:T(128)} %param.5) | copy-start | bytes 388
  5.6 44.2 %all-to-all-start = ((bf16[32,3,128,64]{2,3,1,0:T(8,128)(2,1)}), bf16[32,3,128,64]{2,3,1,0:T(8,128)(2,1)S(1)}, u32[]{:S(2)}, u32[]{:S(2)}) async-start(bf16[32,3,128,64]{2,3,1,0:T(8,128)(2,1)} %broadcast_select_fusion.1), calls=%async_computation | async-start | bytes 3145728 | tf_op jit(solution)/shard_map/all_to_all | solution.py:54
  51.5 75.0 %copy-start.10 = (s32[1,1,12,24]{3,1,2,0:T(1,128)S(1)}, s32[1,1,12,24]{3,1,2,0:T(1,128)}, u32[]{:S(2)}) copy-start(s32[1,1,12,24]{3,1,2,0:T(1,128)} %param.8) | copy-start | bytes 3460
  51.5 37.0 %collective-permute-start = (bf16[1,1,12,128,512]{4,3,2,1,0:T(8,128)(2,1)S(1)}, bf16[1,1,12,128,512]{4,3,2,1,0:T(8,128)(2,1)S(1)}, u32[]{:S(2)}, u32[]{:S(2)}) collective-permute-start(bf16[1,1,12,128,512]{4,3,2,1,0:T(8,128)(2,1)S(1)} %bitcast_select_fusion), channel_id=1, source_target_pairs={{0,8},{8,16},{16,24},{24,0},{1,9},{9,17},{17,25},{25,1},{2,10},{10... | collective-permute-start | bytes 4718600 | tf_op jit(solution)/shard_map/ppermute | solution.py:16
  52.2 69.3 %collective-permute-start.1 = (bf16[1,1,12,128,512]{4,3,2,1,0:T(8,128)(2,1)S(1)}, bf16[1,1,12,128,512]{4,3,2,1,0:T(8,128)(2,1)S(1)}, u32[]{:S(2)}, u32[]{:S(2)}) collective-permute-start(bf16[1,1,12,128,512]{4,3,2,1,0:T(8,128)(2,1)S(1)} %bitcast_select_fusion), channel_id=1, source_target_pairs={{8,0},{16,8},{24,16},{0,24},{9,1},{17,9},{25,17},{1,25},{10,2},{18... | collective-permute-start | bytes 4718600 | tf_op jit(solution)/shard_map/ppermute | solution.py:18
  88.5 33.0 %copy-start.3 = (bf16[1,1,12,128,512]{4,3,2,1,0:T(8,128)(2,1)}, bf16[1,1,12,128,512]{4,3,2,1,0:T(8,128)(2,1)S(1)}, u32[]{:S(2)}) copy-start(bf16[1,1,12,128,512]{4,3,2,1,0:T(8,128)(2,1)S(1)} %collective-permute-done) | copy-start | bytes 4718596
  121.5 2.7 copy-start.4
  124.2 102.5 %collective-permute-start.2 = (bf16[3,1,12,128,512]{4,3,2,1,0:T(8,128)(2,1)}, bf16[3,1,12,128,512]{4,3,2,1,0:T(8,128)(2,1)}, u32[]{:S(2)}, u32[]{:S(2)}) collective-permute-start(bf16[3,1,12,128,512]{4,3,2,1,0:T(8,128)(2,1)} %pad_maximum_fusion.3), channel_id=1, source_target_pairs={{0,1},{1,2},{2,3},{3,4},{4,5},{5,6},{6,7},{7,0},{8,9},{9,10},{10,1... | collective-permute-start | bytes 14155784 | tf_op jit(solution)/shard_map/ppermute | solution.py:16
  126.5 102.8 %collective-permute-start.3 = (bf16[3,1,12,128,512]{4,3,2,1,0:T(8,128)(2,1)}, bf16[3,1,12,128,512]{4,3,2,1,0:T(8,128)(2,1)}, u32[]{:S(2)}, u32[]{:S(2)}) collective-permute-start(bf16[3,1,12,128,512]{4,3,2,1,0:T(8,128)(2,1)} %pad_maximum_fusion.3), channel_id=1, source_target_pairs={{1,0},{2,1},{3,2},{4,3},{5,4},{6,5},{7,6},{0,7},{9,8},{10,9},{11,1... | collective-permute-start | bytes 14155784 | tf_op jit(solution)/shard_map/ppermute | solution.py:18
  279.1 73.1 %copy-start.2 = (f32[12,512,128,1]{2,1,3,0:T(8,128)}, f32[12,512,128,1]{2,1,3,0:T(8,128)S(1)}, u32[]{:S(2)}) copy-start(f32[12,512,128,1]{2,1,3,0:T(8,128)S(1)} %fusion.4) | copy-start | bytes 9437188
  279.5 37.6 %collective-permute-start.4 = (bf16[1,1,12,128,512]{3,4,2,1,0:T(8,128)(2,1)S(1)}, bf16[1,1,12,128,512]{3,4,2,1,0:T(8,128)(2,1)S(1)}, u32[]{:S(2)}, u32[]{:S(2)}) collective-permute-start(bf16[1,1,12,128,512]{3,4,2,1,0:T(8,128)(2,1)S(1)} %fusion.19), channel_id=1, source_target_pairs={{0,8},{8,16},{16,24},{24,0},{1,9},{9,17},{17,25},{25,1},{2,10},{10... | collective-permute-start | bytes 4718600 | tf_op jit(solution)/shard_map/ppermute | solution.py:16
  280.4 69.1 %collective-permute-start.5 = (bf16[1,1,12,128,512]{3,4,2,1,0:T(8,128)(2,1)S(1)}, bf16[1,1,12,128,512]{3,4,2,1,0:T(8,128)(2,1)S(1)}, u32[]{:S(2)}, u32[]{:S(2)}) collective-permute-start(bf16[1,1,12,128,512]{3,4,2,1,0:T(8,128)(2,1)S(1)} %fusion.19), channel_id=1, source_target_pairs={{8,0},{16,8},{24,16},{0,24},{9,1},{17,9},{25,17},{1,25},{10,2},{18... | collective-permute-start | bytes 4718600 | tf_op jit(solution)/shard_map/ppermute | solution.py:18
  317.0 35.1 %copy-start.5 = (bf16[1,1,12,128,512]{3,4,2,1,0:T(8,128)(2,1)}, bf16[1,1,12,128,512]{3,4,2,1,0:T(8,128)(2,1)S(1)}, u32[]{:S(2)}) copy-start(bf16[1,1,12,128,512]{3,4,2,1,0:T(8,128)(2,1)S(1)} %collective-permute-done.4) | copy-start | bytes 4718596
  349.5 2.7 copy-start.6
  352.2 99.3 %collective-permute-start.6 = (bf16[3,1,12,128,512]{3,4,2,1,0:T(8,128)(2,1)}, bf16[3,1,12,128,512]{3,4,2,1,0:T(8,128)(2,1)}, u32[]{:S(2)}, u32[]{:S(2)}) collective-permute-start(bf16[3,1,12,128,512]{3,4,2,1,0:T(8,128)(2,1)} %pad_maximum_fusion.4), channel_id=1, source_target_pairs={{0,1},{1,2},{2,3},{3,4},{4,5},{5,6},{6,7},{7,0},{8,9},{9,10},{10,1... | collective-permute-start | bytes 14155784 | tf_op jit(solution)/shard_map/ppermute | solution.py:16
  353.1 103.9 %collective-permute-start.7 = (bf16[3,1,12,128,512]{3,4,2,1,0:T(8,128)(2,1)}, bf16[3,1,12,128,512]{3,4,2,1,0:T(8,128)(2,1)}, u32[]{:S(2)}, u32[]{:S(2)}) collective-permute-start(bf16[3,1,12,128,512]{3,4,2,1,0:T(8,128)(2,1)} %pad_maximum_fusion.4), channel_id=1, source_target_pairs={{1,0},{2,1},{3,2},{4,3},{5,4},{6,5},{7,6},{0,7},{9,8},{10,9},{11,1... | collective-permute-start | bytes 14155784 | tf_op jit(solution)/shard_map/ppermute | solution.py:18
  467.2 20.5 %copy-start.7 = (bf16[12,128,512]{1,2,0:T(8,128)(2,1)S(1)}, bf16[12,128,512]{1,2,0:T(8,128)(2,1)}, u32[]{:S(2)}) copy-start(bf16[12,128,512]{1,2,0:T(8,128)(2,1)} %copy.23) | copy-start | bytes 4718596
  510.2 73.0 %copy-start.9 = (f32[4]{0:T(128)S(1)}, f32[4]{0:T(128)}, u32[]{:S(2)}) copy-start(f32[4]{0:T(128)} %param.9) | copy-start | bytes 52
  510.3 36.6 %collective-permute-start.8 = (bf16[1,1,12,128,512]{3,4,2,1,0:T(8,128)(2,1)S(1)}, bf16[1,1,12,128,512]{3,4,2,1,0:T(8,128)(2,1)S(1)}, u32[]{:S(2)}, u32[]{:S(2)}) collective-permute-start(bf16[1,1,12,128,512]{3,4,2,1,0:T(8,128)(2,1)S(1)} %convert_bitcast_fusion), channel_id=1, source_target_pairs={{0,8},{8,16},{16,24},{24,0},{1,9},{9,17},{17,25},{25,1},{2,10},{10... | collective-permute-start | bytes 4718600 | tf_op jit(solution)/shard_map/ppermute | solution.py:16
  512.2 69.9 %collective-permute-start.9 = (bf16[1,1,12,128,512]{3,4,2,1,0:T(8,128)(2,1)S(1)}, bf16[1,1,12,128,512]{3,4,2,1,0:T(8,128)(2,1)S(1)}, u32[]{:S(2)}, u32[]{:S(2)}) collective-permute-start(bf16[1,1,12,128,512]{3,4,2,1,0:T(8,128)(2,1)S(1)} %convert_bitcast_fusion), channel_id=1, source_target_pairs={{8,0},{16,8},{24,16},{0,24},{9,1},{17,9},{25,17},{1,25},{10,2},{18... | collective-permute-start | bytes 4718600 | tf_op jit(solution)/shard_map/ppermute | solution.py:18
  582.7 99.2 %collective-permute-start.10 = (bf16[3,1,12,128,512]{3,4,2,1,0:T(8,128)(2,1)S(1)}, bf16[3,1,12,128,512]{3,4,2,1,0:T(8,128)(2,1)S(1)}, u32[]{:S(2)}, u32[]{:S(2)}) collective-permute-start(bf16[3,1,12,128,512]{3,4,2,1,0:T(8,128)(2,1)S(1)} %pad_maximum_fusion.5), channel_id=1, source_target_pairs={{0,1},{1,2},{2,3},{3,4},{4,5},{5,6},{6,7},{7,0},{8,9},{9,10},{10,1... | collective-permute-start | bytes 14155784 | tf_op jit(solution)/shard_map/ppermute | solution.py:16
  583.2 104.2 %collective-permute-start.11 = (bf16[3,1,12,128,512]{3,4,2,1,0:T(8,128)(2,1)S(1)}, bf16[3,1,12,128,512]{3,4,2,1,0:T(8,128)(2,1)S(1)}, u32[]{:S(2)}, u32[]{:S(2)}) collective-permute-start(bf16[3,1,12,128,512]{3,4,2,1,0:T(8,128)(2,1)S(1)} %pad_maximum_fusion.5), channel_id=1, source_target_pairs={{1,0},{2,1},{3,2},{4,3},{5,4},{6,5},{7,6},{0,7},{9,8},{10,9},{11,1... | collective-permute-start | bytes 14155784 | tf_op jit(solution)/shard_map/ppermute | solution.py:18
  713.0 27.3 %copy-start.1 = (bf16[96,1,128,64]{2,3,1,0:T(8,128)(2,1)S(1)}, bf16[96,1,128,64]{2,3,1,0:T(8,128)(2,1)}, u32[]{:S(2)}) copy-start(bf16[96,1,128,64]{2,3,1,0:T(8,128)(2,1)} %param.6) | copy-start | bytes 4718596
where the time goes:
time: 741 us; the launch traced here: 740 us
  waiting for transfers between devices  543 us (73%)
  local copies, waits for them, and re-layouts  72.1 us (10%)
  matrix products  63.2 us (9%)
  other arithmetic  39.9 us (5%)
  starting transfers between devices  21.6 us (3%)
    ppermute x6, waiting for transfers between devices, extended(): lax.ppermute(tail, axis, [(i, (i + 1) % count) for i in range(count)])  395 us
    ppermute x6, waiting for transfers between devices, extended(): lax.ppermute(head, axis, [((i + 1) % count, i) for i in range(count)])  114 us
    dot_general x3, matrix products, operate(): jnp.einsum('rkab,rkbw->raw', local_blocks, all_pieces, preferred_element_...  63.2 us
    gather x3, local copies, waits for them, and re-layouts, operate(): all_pieces = flat_halo[halo_index]  61.4 us
    all_to_all x1, waiting for transfers between devices, local(): lax.all_to_all(outgoing, ('gx', 'gy'), split_axis=0, concat_axis=3, tiled...  34.4 us
    concatenate x6, other arithmetic, extended(): jnp.concatenate([lax.ppermute(tail, axis, [(i, (i + 1) % count) for i in...  31.4 us
  transfers between devices with their start and end apart: 13, of which 13 were waited for; matrix products, arithmetic and copies ran while one was open for 1% of the time, Pallas kernels for 0%

commit v1 on v0

v1 whole, which is shorter than its diff:
```python
import functools

import jax
import jax.numpy as jnp
from jax import lax
from jax.experimental import pallas as pl
from jax.experimental.pallas import tpu as pltpu
from jax.sharding import PartitionSpec as P

OWN = 4
BASE = 7


def pack_kernel(first_ref, held_ref, out_ref, sem):
    slots = held_ref.shape[0]
    domains, per_peer = out_ref.shape[:2]
    for d in range(domains):
        for t in range(per_peer):
            slot = jnp.minimum(first_ref[d] + t, slots - 1)
            pltpu.make_async_copy(held_ref.at[slot], out_ref.at[d, t], sem).start()
    pltpu.make_async_copy(out_ref, out_ref, sem).wait()


def pack(first_slot, held, per_peer):
    return pl.pallas_call(
        pack_kernel,
        out_shape=jax.ShapeDtypeStruct((first_slot.shape[0], per_peer) + held.shape[1:], held.dtype),
        grid_spec=pltpu.PrefetchScalarGridSpec(
            num_scalar_prefetch=1,
            grid=(1,),
            in_specs=[pl.BlockSpec(memory_space=pl.ANY)],
            out_specs=pl.BlockSpec(memory_space=pl.ANY),
            scratch_shapes=[pltpu.SemaphoreType.DMA],
        ),
        name="pack",
    )(first_slot, held)


def step_kernel(mode, base, extras, meta_ref, pattern_ref, coeffs_ref, *refs):
    pieces, refs = refs[:9], refs[9:]
    overflow, refs = refs[:extras], refs[extras:]
    blocks_ref, refs = refs[0], refs[1:]
    halo, acc, sems = refs[-3:]
    refs = refs[:-3]
    r = pl.program_id(0)
    count = meta_ref[0]
    capacity, slots = pattern_ref.shape

    def piece_copy(c):
        size = pieces[c].shape[0]
        return pltpu.make_async_copy(pieces[c], halo.at[pl.ds(c * capacity, size)], sems.at[c])

    def extra_copy(h):
        code = meta_ref[1 + h]
        return pltpu.make_async_copy(
            overflow[h], halo.at[pl.ds(code * capacity + base, capacity - base)], sems.at[9 + h]
        )

    @pl.when(r == 0)
    def _():
        for c in range(9):
            piece_copy(c).start()
        for h in range(extras):
            pl.when(meta_ref[1 + h] >= 0)(lambda h=h: extra_copy(h).start())
        for c in range(9):
            piece_copy(c).wait()
        for h in range(extras):
            pl.when(meta_ref[1 + h] >= 0)(lambda h=h: extra_copy(h).wait())

    @pl.when(r < count)
    def _():
        for k in range(0, slots, 2):
            lhs = jnp.concatenate([blocks_ref[0, k], blocks_ref[0, k + 1]], axis=1)
            rhs = jnp.concatenate([halo[pattern_ref[r, k]], halo[pattern_ref[r, k + 1]]], axis=0)
            part = jnp.dot(lhs, rhs, preferred_element_type=jnp.float32)
            if k == 0:
                acc[...] = part
            else:
                acc[...] += part
        total = acc[...]
        if mode == 1:
            sent_ref, cheb_ref = refs
            cheb_ref[0] = total
            sent_ref[0] = total.astype(sent_ref.dtype)
        elif mode == 2:
            start_ref, sent_ref, cheb_ref = refs
            cheb = 2.0 * total - start_ref[0].astype(jnp.float32)
            cheb_ref[0] = cheb
            sent_ref[0] = cheb.astype(sent_ref.dtype)
        else:
            start_ref, one_ref, two_ref, out_ref = refs
            one = one_ref[0]
            out_ref[0] = (
                coeffs_ref[0] * start_ref[0].astype(jnp.float32)
                + coeffs_ref[1] * one
                + coeffs_ref[2] * two_ref[0]
                + coeffs_ref[3] * (2.0 * total - one)
            )

    @pl.when(r >= count)
    def _():
        for ref in refs if mode == 1 else refs[1:] if mode == 2 else refs[3:]:
            ref[...] = jnp.zeros_like(ref)


def step(mode, base, meta, pattern, coeffs, pieces, overflow, blocks, panels):
    capacity, slots = pattern.shape
    rows, cols = pieces[0].shape[1:]

    def live(r, meta, pattern):
        return jnp.minimum(r, meta[0] - 1)

    panel_in = pl.BlockSpec((1, rows, cols), lambda r, m, p: (live(r, m, p), 0, 0))
    panel_out = pl.BlockSpec((1, rows, cols), lambda r, m, p: (r, 0, 0))
    shape = (capacity, rows, cols)
    wide = jax.ShapeDtypeStruct(shape, jnp.float32)
    narrow = jax.ShapeDtypeStruct(shape, jnp.bfloat16)
    outs = [wide] if mode == 3 else [narrow, wide]
    return pl.pallas_call(
        functools.partial(step_kernel, mode, base, len(overflow)),
        out_shape=outs,
        grid_spec=pltpu.PrefetchScalarGridSpec(
            num_scalar_prefetch=2,
            grid=(capacity,),
            in_specs=[pl.BlockSpec(memory_space=pltpu.SMEM)]
            + [pl.BlockSpec(memory_space=pl.ANY)] * (9 + len(overflow))
            + [pl.BlockSpec((1, slots, rows, rows), lambda r, m, p: (live(r, m, p), 0, 0, 0))]
            + [panel_in] * len(panels),
            out_specs=[panel_out] * len(outs),
            scratch_shapes=[
                pltpu.VMEM((9 * capacity, rows, cols), jnp.bfloat16),
                pltpu.VMEM((rows, cols), jnp.float32),
                pltpu.SemaphoreType.DMA((9 + len(overflow),)),
            ],
        ),
        compiler_params=pltpu.CompilerParams(vmem_limit_bytes=40 * 1024 * 1024),
        name=f"step{mode}",
    )(meta, pattern, coeffs, *pieces, *overflow, blocks, *panels)


def shifted(x, axis, by):
    count = lax.axis_size(axis)
    return lax.ppermute(x, axis, [(i, (i + by) % count) for i in range(count)])


def halo_pieces(panels, base):
    own = panels[:base]
    above, below = shifted(own, "gx", 1), shifted(own, "gx", -1)
    left, right = shifted(own, "gy", 1), shifted(own, "gy", -1)
    return [
        shifted(above, "gy", 1), above, shifted(above, "gy", -1),
        left, panels, right,
        shifted(below, "gy", 1), below, shifted(below, "gy", -1),
    ]


def local(counts, probes, blocks, pattern, coeffs):
    grid_rows = lax.axis_size("gx")
    grid_cols = lax.axis_size("gy")
    domains = grid_rows * grid_cols
    capacity = blocks.shape[2]
    panel_rows = blocks.shape[4]
    probe_cols = probes.shape[3] * grid_cols
    per_peer = (capacity + grid_rows - 1) // grid_rows
    my_row, my_col = lax.axis_index("gx"), lax.axis_index("gy")
    my_domain = my_row * grid_cols + my_col
    ids = jnp.arange(domains, dtype=jnp.int32)
    offsets = jnp.sum(jnp.where(ids[None, :] < ids[:, None], counts[None, :], 0), axis=1)
    my_count = jnp.sum(jnp.where(ids == my_domain, counts, 0))
    my_offset = jnp.sum(jnp.where(ids < my_domain, counts, 0))
    first_slot = (offsets + (my_row - offsets) % grid_rows) // grid_rows
    outgoing = pack(first_slot, probes[:, 0], per_peer)
    arrived = lax.all_to_all(outgoing, ("gx", "gy"), split_axis=0, concat_axis=3, tiled=True)
    arrived = arrived.reshape(per_peer, panel_rows, grid_rows, probe_cols).transpose(0, 2, 1, 3)
    arrived = jnp.concatenate([arrived, arrived], axis=1)
    start = lax.dynamic_slice_in_dim(arrived, my_offset % grid_rows, grid_rows, axis=1)
    start = start.reshape(per_peer * grid_rows, panel_rows, probe_cols)[:capacity]
    rows, table = blocks[0, 0], pattern[0, 0]

    def expand(base, heavy, start):
        meta = [my_count]
        for d in heavy:
            di = (d // grid_cols - my_row + 1) % grid_rows
            dj = (d % grid_cols - my_col + 1) % grid_cols
            near = (d >= 0) & (di < 3) & (dj < 3) & (d != my_domain)
            meta.append(jnp.where(near, di * 3 + dj, -1))
        meta = jnp.stack(meta).astype(jnp.int32)

        def run(mode, panels, *rest):
            overflow = [
                lax.psum(
                    jnp.where(d == my_domain, panels[base:], jnp.zeros((), panels.dtype)), ("gx", "gy")
                )
                for d in heavy
            ]
            pieces = halo_pieces(panels, base)
            return step(mode, base, meta, table, coeffs, pieces, overflow, rows, rest)

        sent, one = run(1, start)
        sent, two = run(2, sent, start)
        (out,) = run(3, sent, start, one, two)
        return out

    base = min(BASE, capacity)
    extras = max(1, domains // 32)
    over = counts > base
    rank = jnp.sum(jnp.where(ids[None, :] < ids[:, None], over[None, :], False), axis=1)
    heavy = [jnp.max(jnp.where(over & (rank == h), ids, -1)) for h in range(extras)]
    out = lax.cond(
        jnp.sum(over) <= extras,
        lambda s: expand(base, heavy, s),
        lambda s: expand(capacity, [], s),
        start,
    )
    return out[None, None]


def solution(mesh):
    in_specs = (
        P(),
        P(None, "gx", None, "gy"),
        P("gx", "gy", None, None, None, None),
        P("gx", "gy", None, None),
        P(),
    )
    out_specs = P("gx", "gy", None, None, None)
    return jax.shard_map(local, mesh=mesh, in_specs=in_specs, out_specs=out_specs, check_vma=False)
```

time: 741 us -> 753 us (1.016); the launches traced: 740 us -> 742 us
  Pallas kernels: 0 us -> 120 us
  matrix products: 63.2 us -> 0 us
  waiting for transfers between devices: 543 us -> 490 us
  starting transfers between devices: 21.6 us -> 68.1 us
  local copies, waits for them, and re-layouts: 72.1 us -> 35.3 us
  other arithmetic: 39.9 us -> 7.88 us
  between operations: 0.21 us -> 15.6 us
    ppermute x12 -> x24, waiting for transfers between devices: 509 us -> 77.8 us  [shifted(): return lax.ppermute(x, axis, [(i, (i + by) % count) for i in range(count)])]
    psum x0 -> x3, waiting for transfers between devices: none -> 378 us  [run(): lax.psum(jnp.where(d == my_domain, panels[base:], jnp.zeros((), panels.dt...]
    pallas_call x0 -> x4, Pallas kernels: none -> 120 us  [the longest x1 97.1 us: pack(): pl.pallas_call(pack_kernel, out_shape=jax.ShapeDtypeStruct((first_slot.sh...]
    gather x6 -> x0, local copies, waits for them, and re-layouts: 64.4 us -> none  [the longest x3 61.4 us: operate(): all_pieces = flat_halo[halo_index]]
    dot_general x3 -> x0, matrix products: 63.2 us -> none  [operate(): jnp.einsum('rkab,rkbw->raw', local_blocks, all_pieces, preferred_element_...]
    ppermute x12 -> x24, starting transfers between devices: 14.6 us -> 60.9 us  [shifted(): return lax.ppermute(x, axis, [(i, (i + by) % count) for i in range(count)])]
    concatenate x7 -> x1, other arithmetic: 32.1 us -> 0.58 us  [local(): arrived = jnp.concatenate([arrived, arrived], axis=1)]
    cond x0 -> x36, local copies, waits for them, and re-layouts: none -> 19.2 us
  transfers between devices with their start and end apart: 13 -> 28, of which waited for: 13 -> 9; matrix products, arithmetic and copies ran while one was open for 1% -> 1% of each run, Pallas kernels for 0% -> 0%
where the time goes in v1:
time: 753 us; the launch traced here: 742 us
  waiting for transfers between devices  490 us (65%)
  Pallas kernels  120 us (16%)
  starting transfers between devices  68.1 us (9%)
  local copies, waits for them, and re-layouts  35.3 us (5%)
  between operations  15.6 us (2%)
  other arithmetic  7.88 us (1%)
    psum x3, waiting for transfers between devices, run(): lax.psum(jnp.where(d == my_domain, panels[base:], jnp.zeros((), panels.dt...  378 us
    pallas_call x1, Pallas kernels, pack(): pl.pallas_call(pack_kernel, out_shape=jax.ShapeDtypeStruct((first_slot.sh...  97.1 us
    ppermute x24, waiting for transfers between devices, shifted(): return lax.ppermute(x, axis, [(i, (i + by) % count) for i in range(count)])  77.8 us
    ppermute x24, starting transfers between devices, shifted(): return lax.ppermute(x, axis, [(i, (i + by) % count) for i in range(count)])  60.9 us
    all_to_all x1, waiting for transfers between devices, local(): lax.all_to_all(outgoing, ('gx', 'gy'), split_axis=0, concat_axis=3, tiled...  34.6 us
    pallas_call x3, Pallas kernels, step(): pl.pallas_call(functools.partial(step_kernel, mode, base, len(overflow)),...  23 us
    cond x36, local copies, waits for them, and re-layouts  19.2 us
  transfers between devices with their start and end apart: 28, of which 9 were waited for; matrix products, arithmetic and copies ran while one was open for 1% of the time, Pallas kernels for 0%

profile of v1, /device:TPU:1, one launch (start us, length us, event | category | flops | bytes accessed | tf_op | source)
XLA Modules:
  0.0 742.0 jit_solution(13941408614909258267)
XLA Ops:
  7.3 4.1 copy.14
  12.7 97.1 %pack.1 = bf16[32,3,128,64]{3,2,1,0:T(8,128)(2,1)} custom-call(s32[32]{0:T(128)} %get-tuple-element.82.first_ref, bf16[96,128,64]{2,1,0:T(8,128)(2,1)} %bitcast.20), custom_call_target="tpu_custom_call" | custom-call | tf_op jit(solution)/shard_map/pack/pallas_call | solution.py:25
  109.8 4.3 copy.15
  114.1 7.1 all-to-all-start
  123.7 34.6 %all-to-all-done = bf16[32,3,128,64]{2,3,1,0:T(8,128)(2,1)S(1)} async-done(((bf16[32,3,128,64]{2,3,1,0:T(8,128)(2,1)}), bf16[32,3,128,64]{2,3,1,0:T(8,128)(2,1)S(1)}, u32[]{:S(2)}, u32[]{:S(2)}) %all-to-all-start) | async-done | bytes 1572896 | tf_op jit(solution)/shard_map/all_to_all | solution.py:173
  160.6 573.2 %conditional.1 = (f32[1,1,12,128,512]{4,3,2,1,0:T(8,128)S(1)}) conditional(s32[]{:T(128)} %convert_element_type.10, (s32[]{:T(128)}, bf16[12,128,512]{2,1,0:T(8,128)(2,1)}, s32[12,24]{1,0:T(8,128)S(1)}, f32[4]{0:T(128)S(1)}, bf16[12,24,128,128]{3,2,1,0:T(8,128)(2,1)}) %tuple.37, (s32[]{:T(128)}, s32[32,32]{1,0:T(8,128)S(1)}, s32[32]{0:T(128)S(1)}, ...), branch_computations={%region_4.5_spmd, %region_5.11_spmd} | conditional | flops 1967257 | bytes 198974208 | solution.py:209
  166.6 17.5 %collective-permute-done.29.refs_7_ = bf16[7,128,512]{2,1,0:T(8,128)(2,1)S(1)} collective-permute-done((bf16[7,128,512]{2,1,0:T(8,128)(2,1)}, bf16[7,128,512]{2,1,0:T(8,128)(2,1)S(1)}, u32[]{:S(2)}, u32[]{:S(2)}) %collective-permute-start.29) | collective-permute-done | bytes 917536 | tf_op jit(solution)/shard_map/cond/branch_1_fun/ppermute | solution.py:143
  186.3 20.1 %collective-permute-start.30 = (bf16[7,128,512]{2,1,0:T(8,128)(2,1)S(1)}, bf16[7,128,512]{2,1,0:T(8,128)(2,1)}, u32[]{:S(2)}, u32[]{:S(2)}) collective-permute-start(bf16[7,128,512]{2,1,0:T(8,128)(2,1)S(1)} %collective-permute-done.29.refs_7_), channel_id=1, source_target_pairs={{0,1},{1,2},{2,3},{3,4},{4,5},{5,6},{6,7},{7,0},{8,9},{9,10},{10,1... | collective-permute-start | bytes 2752520 | tf_op jit(solution)/shard_map/cond/branch_1_fun/ppermute | solution.py:143
  217.0 122.8 %all-reduce.4.cloned.1.call-done.refs_9_ = bf16[5,128,512]{2,1,0:T(8,128)(2,1)} async-done(((bf16[5,128,512]{2,1,0:T(8,128)(2,1)}), bf16[5,128,512]{2,1,0:T(8,128)(2,1)}) %all-reduce.4.cloned.1.call-update) | async-done | bytes 655376 | tf_op jit(solution)/shard_map/cond/branch_1_fun/psum | solution.py:191
  345.3 7.6 %step1.3 = (bf16[12,128,512]{2,1,0:T(8,128)(2,1)S(1)}, f32[12,128,512]{2,1,0:T(8,128)S(1)}) custom-call(s32[2]{0:T(128)S(1)} %pad_add_fusion.meta_ref, s32[12,24]{1,0:T(8,128)S(1)} %get-tuple-element.70.pattern_ref, f32[4]{0:T(128)S(1)} %get-tuple-element.71.coeffs_ref, bf16[7,128,512]{2,1,0:T(8,128)(2,1)} %collective-permute-done.25.refs_0_, ...), custom_call_target="tpu_custom_call" | custom-call | tf_op jit(solution)/shard_map/cond/branch_1_fun/step1/pallas_call | solution.py:119
  359.0 2.9 collective-permute-start.36
  363.5 13.8 %collective-permute-done.37.refs_7_ = bf16[7,128,512]{2,1,0:T(8,128)(2,1)S(1)} collective-permute-done((bf16[7,128,512]{2,1,0:T(8,128)(2,1)}, bf16[7,128,512]{2,1,0:T(8,128)(2,1)S(1)}, u32[]{:S(2)}, u32[]{:S(2)}) %collective-permute-start.37) | collective-permute-done | bytes 917536 | tf_op jit(solution)/shard_map/cond/branch_1_fun/ppermute | solution.py:143
  377.3 4.0 collective-permute-start.39
  383.2 16.4 %collective-permute-done.32.refs_1_ = bf16[7,128,512]{2,1,0:T(8,128)(2,1)} collective-permute-done((bf16[7,128,512]{2,1,0:T(8,128)(2,1)}, bf16[7,128,512]{2,1,0:T(8,128)(2,1)}, u32[]{:S(2)}, u32[]{:S(2)}) %collective-permute-start.32) | collective-permute-done | bytes 917536 | tf_op jit(solution)/shard_map/cond/branch_1_fun/ppermute | solution.py:143
  400.5 2.8 collective-permute-start.33
  404.3 127.5 %all-reduce.6.cloned.1.call-done.refs_9_ = bf16[5,128,512]{2,1,0:T(8,128)(2,1)} async-done(((bf16[5,128,512]{2,1,0:T(8,128)(2,1)}), bf16[5,128,512]{2,1,0:T(8,128)(2,1)}) %all-reduce.6.cloned.1.call-update) | async-done | bytes 655376 | tf_op jit(solution)/shard_map/cond/branch_1_fun/psum | solution.py:191
  535.4 7.7 %step2.3 = (bf16[12,128,512]{2,1,0:T(8,128)(2,1)S(1)}, f32[12,128,512]{2,1,0:T(8,128)S(1)}) custom-call(s32[2]{0:T(128)S(1)} %pad_add_fusion.meta_ref, s32[12,24]{1,0:T(8,128)S(1)} %get-tuple-element.70.pattern_ref, f32[4]{0:T(128)S(1)} %get-tuple-element.71.coeffs_ref, bf16[7,128,512]{2,1,0:T(8,128)(2,1)} %collective-permute-done.33.refs_0_, ...), custom_call_target="tpu_custom_call" | custom-call | tf_op jit(solution)/shard_map/cond/branch_1_fun/step2/pallas_call | solution.py:119
  549.0 2.9 collective-permute-start.44
  553.6 13.8 %collective-permute-done.45.refs_7_ = bf16[7,128,512]{2,1,0:T(8,128)(2,1)S(1)} collective-permute-done((bf16[7,128,512]{2,1,0:T(8,128)(2,1)}, bf16[7,128,512]{2,1,0:T(8,128)(2,1)S(1)}, u32[]{:S(2)}, u32[]{:S(2)}) %collective-permute-start.45) | collective-permute-done | bytes 917536 | tf_op jit(solution)/shard_map/cond/branch_1_fun/ppermute | solution.py:143
  567.3 4.0 collective-permute-start.47
  573.2 16.3 %collective-permute-done.40.refs_1_ = bf16[7,128,512]{2,1,0:T(8,128)(2,1)S(1)} collective-permute-done((bf16[7,128,512]{2,1,0:T(8,128)(2,1)}, bf16[7,128,512]{2,1,0:T(8,128)(2,1)S(1)}, u32[]{:S(2)}, u32[]{:S(2)}) %collective-permute-start.40) | collective-permute-done | bytes 917536 | tf_op jit(solution)/shard_map/cond/branch_1_fun/ppermute | solution.py:143
  590.4 2.8 collective-permute-start.41
  594.2 127.7 %all-reduce.8.cloned.1.call-done.refs_9_ = bf16[5,128,512]{2,1,0:T(8,128)(2,1)} async-done(((bf16[5,128,512]{2,1,0:T(8,128)(2,1)}), bf16[5,128,512]{2,1,0:T(8,128)(2,1)}) %all-reduce.8.cloned.1.call-update) | async-done | bytes 655376 | tf_op jit(solution)/shard_map/cond/branch_1_fun/psum | solution.py:191
  726.1 7.7 %step3.3 = f32[12,128,512]{2,1,0:T(8,128)S(1)} custom-call(s32[2]{0:T(128)S(1)} %pad_add_fusion.meta_ref, s32[12,24]{1,0:T(8,128)S(1)} %get-tuple-element.70.pattern_ref, f32[4]{0:T(128)S(1)} %get-tuple-element.71.coeffs_ref, bf16[7,128,512]{2,1,0:T(8,128)(2,1)} %collective-permute-done.41.refs_0_, bf16[7,128,512]{2,1,0:T(8,128)(2,1)S(1)} %collective-permute-done.40.refs_1_, ...), custom_call_target="tpu_custom_call" | custom-call | tf_op jit(solution)/shard_map/cond/branch_1_fun/step3/pallas_call | solution.py:119
  (106 shorter events, 56.4 us)
Async XLA Ops:
  114.1 44.2 %all-to-all-start = ((bf16[32,3,128,64]{2,3,1,0:T(8,128)(2,1)}), bf16[32,3,128,64]{2,3,1,0:T(8,128)(2,1)S(1)}, u32[]{:S(2)}, u32[]{:S(2)}) async-start(bf16[32,3,128,64]{2,3,1,0:T(8,128)(2,1)} %copy.15), calls=%async_computation | async-start | bytes 3145728 | tf_op jit(solution)/shard_map/all_to_all | solution.py:173
  160.7 179.1 %all-reduce.4.cloned.1.call-start = ((), (), s32[]{:S(2)}) async-start(), calls=%async_computation.1 | async-start | bytes 1310720 | tf_op jit(solution)/shard_map/cond/branch_1_fun/psum | solution.py:191
  164.5 41.9 %collective-permute-start.24 = (bf16[7,128,512]{2,1,0:T(8,128)(2,1)}, bf16[7,128,512]{2,1,0:T(8,128)(2,1)S(1)}, u32[]{:S(2)}, u32[]{:S(2)}) collective-permute-start(bf16[7,128,512]{2,1,0:T(8,128)(2,1)} %slice.12), channel_id=1, source_target_pairs={{0,8},{8,16},{16,24},{24,0},{1,9},{9,17},{17,25},{25,1},{2,10},{10... | collective-permute-start | bytes 2752520 | tf_op jit(solution)/shard_map/cond/branch_1_fun/ppermute | solution.py:143
  164.5 41.9 %collective-permute-start.28 = (bf16[7,128,512]{2,1,0:T(8,128)(2,1)}, bf16[7,128,512]{2,1,0:T(8,128)(2,1)S(1)}, u32[]{:S(2)}, u32[]{:S(2)}) collective-permute-start(bf16[7,128,512]{2,1,0:T(8,128)(2,1)} %slice.12), channel_id=1, source_target_pairs={{0,7},{1,0},{2,1},{3,2},{4,3},{5,4},{6,5},{7,6},{8,15},{9,8},{10,9... | collective-permute-start | bytes 2752520 | tf_op jit(solution)/shard_map/cond/branch_1_fun/ppermute | solution.py:143
  165.8 174.0 %collective-permute-start.27 = (bf16[7,128,512]{2,1,0:T(8,128)(2,1)}, bf16[7,128,512]{2,1,0:T(8,128)(2,1)S(1)}, u32[]{:S(2)}, u32[]{:S(2)}) collective-permute-start(bf16[7,128,512]{2,1,0:T(8,128)(2,1)} %slice.12), channel_id=1, source_target_pairs={{0,1},{1,2},{2,3},{3,4},{4,5},{5,6},{6,7},{7,0},{8,9},{9,10},{10,1... | collective-permute-start | bytes 2752520 | tf_op jit(solution)/shard_map/cond/branch_1_fun/ppermute | solution.py:143
  184.1 156.6 %collective-permute-start.31 = (bf16[7,128,512]{2,1,0:T(8,128)(2,1)S(1)}, bf16[7,128,512]{2,1,0:T(8,128)(2,1)}, u32[]{:S(2)}, u32[]{:S(2)}) collective-permute-start(bf16[7,128,512]{2,1,0:T(8,128)(2,1)S(1)} %collective-permute-done.29.refs_7_), channel_id=1, source_target_pairs={{0,7},{1,0},{2,1},{3,2},{4,3},{5,4},{6,5},{7,6},{8,15},{9,8},{10,9... | collective-permute-start | bytes 2752520 | tf_op jit(solution)/shard_map/cond/branch_1_fun/ppermute | solution.py:143
  186.3 154.4 %collective-permute-start.30 = (bf16[7,128,512]{2,1,0:T(8,128)(2,1)S(1)}, bf16[7,128,512]{2,1,0:T(8,128)(2,1)}, u32[]{:S(2)}, u32[]{:S(2)}) collective-permute-start(bf16[7,128,512]{2,1,0:T(8,128)(2,1)S(1)} %collective-permute-done.29.refs_7_), channel_id=1, source_target_pairs={{0,1},{1,2},{2,3},{3,4},{4,5},{5,6},{6,7},{7,0},{8,9},{9,10},{10,1... | collective-permute-start | bytes 2752520 | tf_op jit(solution)/shard_map/cond/branch_1_fun/ppermute | solution.py:143
  206.3 134.3 %collective-permute-start.26 = (bf16[7,128,512]{2,1,0:T(8,128)(2,1)S(1)}, bf16[7,128,512]{2,1,0:T(8,128)(2,1)}, u32[]{:S(2)}, u32[]{:S(2)}) collective-permute-start(bf16[7,128,512]{2,1,0:T(8,128)(2,1)S(1)} %collective-permute-done.24.refs_1_), channel_id=1, source_target_pairs={{0,7},{1,0},{2,1},{3,2},{4,3},{5,4},{6,5},{7,6},{8,15},{9,8},{10,9... | collective-permute-start | bytes 2752520 | tf_op jit(solution)/shard_map/cond/branch_1_fun/ppermute | solution.py:143
  207.4 133.3 %collective-permute-start.25 = (bf16[7,128,512]{2,1,0:T(8,128)(2,1)S(1)}, bf16[7,128,512]{2,1,0:T(8,128)(2,1)}, u32[]{:S(2)}, u32[]{:S(2)}) collective-permute-start(bf16[7,128,512]{2,1,0:T(8,128)(2,1)S(1)} %collective-permute-done.24.refs_1_), channel_id=1, source_target_pairs={{0,1},{1,2},{2,3},{3,4},{4,5},{5,6},{6,7},{7,0},{8,9},{9,10},{10,1... | collective-permute-start | bytes 2752520 | tf_op jit(solution)/shard_map/cond/branch_1_fun/ppermute | solution.py:143
  212.5 319.4 %all-reduce.6.cloned.1.call-start = ((), (), s32[]{:S(2)}) async-start(), calls=%async_computation.2 | async-start | bytes 1310720 | tf_op jit(solution)/shard_map/cond/branch_1_fun/psum | solution.py:191
  356.8 42.8 %collective-permute-start.32 = (bf16[7,128,512]{2,1,0:T(8,128)(2,1)}, bf16[7,128,512]{2,1,0:T(8,128)(2,1)}, u32[]{:S(2)}, u32[]{:S(2)}) collective-permute-start(bf16[7,128,512]{2,1,0:T(8,128)(2,1)} %slice.14), channel_id=1, source_target_pairs={{0,8},{8,16},{16,24},{24,0},{1,9},{9,17},{17,25},{25,1},{2,10},{10... | collective-permute-start | bytes 2752520 | tf_op jit(solution)/shard_map/cond/branch_1_fun/ppermute | solution.py:143
  359.0 40.6 %collective-permute-start.36 = (bf16[7,128,512]{2,1,0:T(8,128)(2,1)}, bf16[7,128,512]{2,1,0:T(8,128)(2,1)S(1)}, u32[]{:S(2)}, u32[]{:S(2)}) collective-permute-start(bf16[7,128,512]{2,1,0:T(8,128)(2,1)} %slice.14), channel_id=1, source_target_pairs={{0,7},{1,0},{2,1},{3,2},{4,3},{5,4},{6,5},{7,6},{8,15},{9,8},{10,9... | collective-permute-start | bytes 2752520 | tf_op jit(solution)/shard_map/cond/branch_1_fun/ppermute | solution.py:143
  361.9 170.0 %collective-permute-start.35 = (bf16[7,128,512]{2,1,0:T(8,128)(2,1)}, bf16[7,128,512]{2,1,0:T(8,128)(2,1)}, u32[]{:S(2)}, u32[]{:S(2)}) collective-permute-start(bf16[7,128,512]{2,1,0:T(8,128)(2,1)} %slice.14), channel_id=1, source_target_pairs={{0,1},{1,2},{2,3},{3,4},{4,5},{5,6},{6,7},{7,0},{8,9},{9,10},{10,1... | collective-permute-start | bytes 2752520 | tf_op jit(solution)/shard_map/cond/branch_1_fun/ppermute | solution.py:143
  377.3 154.6 %collective-permute-start.39 = (bf16[7,128,512]{2,1,0:T(8,128)(2,1)S(1)}, bf16[7,128,512]{2,1,0:T(8,128)(2,1)}, u32[]{:S(2)}, u32[]{:S(2)}) collective-permute-start(bf16[7,128,512]{2,1,0:T(8,128)(2,1)S(1)} %collective-permute-done.37.refs_7_), channel_id=1, source_target_pairs={{0,7},{1,0},{2,1},{3,2},{4,3},{5,4},{6,5},{7,6},{8,15},{9,8},{10,9... | collective-permute-start | bytes 2752520 | tf_op jit(solution)/shard_map/cond/branch_1_fun/ppermute | solution.py:143
  381.3 150.6 %collective-permute-start.38 = (bf16[7,128,512]{2,1,0:T(8,128)(2,1)S(1)}, bf16[7,128,512]{2,1,0:T(8,128)(2,1)}, u32[]{:S(2)}, u32[]{:S(2)}) collective-permute-start(bf16[7,128,512]{2,1,0:T(8,128)(2,1)S(1)} %collective-permute-done.37.refs_7_), channel_id=1, source_target_pairs={{0,1},{1,2},{2,3},{3,4},{4,5},{5,6},{6,7},{7,0},{8,9},{9,10},{10,1... | collective-permute-start | bytes 2752520 | tf_op jit(solution)/shard_map/cond/branch_1_fun/ppermute | solution.py:143
  399.6 132.3 %collective-permute-start.34 = (bf16[7,128,512]{2,1,0:T(8,128)(2,1)}, bf16[7,128,512]{2,1,0:T(8,128)(2,1)}, u32[]{:S(2)}, u32[]{:S(2)}) collective-permute-start(bf16[7,128,512]{2,1,0:T(8,128)(2,1)} %collective-permute-done.32.refs_1_), channel_id=1, source_target_pairs={{0,7},{1,0},{2,1},{3,2},{4,3},{5,4},{6,5},{7,6},{8,15},{9,8},{10,9... | collective-permute-start | bytes 2752520 | tf_op jit(solution)/shard_map/cond/branch_1_fun/ppermute | solution.py:143
  400.5 131.4 %collective-permute-start.33 = (bf16[7,128,512]{2,1,0:T(8,128)(2,1)}, bf16[7,128,512]{2,1,0:T(8,128)(2,1)}, u32[]{:S(2)}, u32[]{:S(2)}) collective-permute-start(bf16[7,128,512]{2,1,0:T(8,128)(2,1)} %collective-permute-done.32.refs_1_), channel_id=1, source_target_pairs={{0,1},{1,2},{2,3},{3,4},{4,5},{5,6},{6,7},{7,0},{8,9},{9,10},{10,1... | collective-permute-start | bytes 2752520 | tf_op jit(solution)/shard_map/cond/branch_1_fun/ppermute | solution.py:143
  404.3 317.6 %all-reduce.8.cloned.1.call-start = ((), (), s32[]{:S(2)}) async-start(), calls=%async_computation.3 | async-start | bytes 1310720 | tf_op jit(solution)/shard_map/cond/branch_1_fun/psum | solution.py:191
  546.8 42.7 %collective-permute-start.40 = (bf16[7,128,512]{2,1,0:T(8,128)(2,1)}, bf16[7,128,512]{2,1,0:T(8,128)(2,1)S(1)}, u32[]{:S(2)}, u32[]{:S(2)}) collective-permute-start(bf16[7,128,512]{2,1,0:T(8,128)(2,1)} %slice.16), channel_id=1, source_target_pairs={{0,8},{8,16},{16,24},{24,0},{1,9},{9,17},{17,25},{25,1},{2,10},{10... | collective-permute-start | bytes 2752520 | tf_op jit(solution)/shard_map/cond/branch_1_fun/ppermute | solution.py:143
  551.9 170.0 %collective-permute-start.43 = (bf16[7,128,512]{2,1,0:T(8,128)(2,1)}, bf16[7,128,512]{2,1,0:T(8,128)(2,1)}, u32[]{:S(2)}, u32[]{:S(2)}) collective-permute-start(bf16[7,128,512]{2,1,0:T(8,128)(2,1)} %slice.16), channel_id=1, source_target_pairs={{0,1},{1,2},{2,3},{3,4},{4,5},{5,6},{6,7},{7,0},{8,9},{9,10},{10,1... | collective-permute-start | bytes 2752520 | tf_op jit(solution)/shard_map/cond/branch_1_fun/ppermute | solution.py:143
  567.3 154.6 %collective-permute-start.47 = (bf16[7,128,512]{2,1,0:T(8,128)(2,1)S(1)}, bf16[7,128,512]{2,1,0:T(8,128)(2,1)}, u32[]{:S(2)}, u32[]{:S(2)}) collective-permute-start(bf16[7,128,512]{2,1,0:T(8,128)(2,1)S(1)} %collective-permute-done.45.refs_7_), channel_id=1, source_target_pairs={{0,7},{1,0},{2,1},{3,2},{4,3},{5,4},{6,5},{7,6},{8,15},{9,8},{10,9... | collective-permute-start | bytes 2752520 | tf_op jit(solution)/shard_map/cond/branch_1_fun/ppermute | solution.py:143
  571.3 150.6 %collective-permute-start.46 = (bf16[7,128,512]{2,1,0:T(8,128)(2,1)S(1)}, bf16[7,128,512]{2,1,0:T(8,128)(2,1)}, u32[]{:S(2)}, u32[]{:S(2)}) collective-permute-start(bf16[7,128,512]{2,1,0:T(8,128)(2,1)S(1)} %collective-permute-done.45.refs_7_), channel_id=1, source_target_pairs={{0,1},{1,2},{2,3},{3,4},{4,5},{5,6},{6,7},{7,0},{8,9},{9,10},{10,1... | collective-permute-start | bytes 2752520 | tf_op jit(solution)/shard_map/cond/branch_1_fun/ppermute | solution.py:143
  589.5 132.4 %collective-permute-start.42 = (bf16[7,128,512]{2,1,0:T(8,128)(2,1)S(1)}, bf16[7,128,512]{2,1,0:T(8,128)(2,1)}, u32[]{:S(2)}, u32[]{:S(2)}) collective-permute-start(bf16[7,128,512]{2,1,0:T(8,128)(2,1)S(1)} %collective-permute-done.40.refs_1_), channel_id=1, source_target_pairs={{0,7},{1,0},{2,1},{3,2},{4,3},{5,4},{6,5},{7,6},{8,15},{9,8},{10,9... | collective-permute-start | bytes 2752520 | tf_op jit(solution)/shard_map/cond/branch_1_fun/ppermute | solution.py:143
  590.4 131.5 %collective-permute-start.41 = (bf16[7,128,512]{2,1,0:T(8,128)(2,1)S(1)}, bf16[7,128,512]{2,1,0:T(8,128)(2,1)}, u32[]{:S(2)}, u32[]{:S(2)}) collective-permute-start(bf16[7,128,512]{2,1,0:T(8,128)(2,1)S(1)} %collective-permute-done.40.refs_1_), channel_id=1, source_target_pairs={{0,1},{1,2},{2,3},{3,4},{4,5},{5,6},{6,7},{7,0},{8,9},{9,10},{10,1... | collective-permute-start | bytes 2752520 | tf_op jit(solution)/shard_map/cond/branch_1_fun/ppermute | solution.py:143
  (26 other events, 430.3 us)
Sparse Core Ops, SparseCore 0:
  212.6 127.0 all-reduce.3
  404.4 127.4 all-reduce.5
  594.4 127.4 all-reduce.7

commit v2 on v1

--- a/solution.py
+++ b/solution.py
@@ -11,34 +11,32 @@
 BASE = 7
 
 
-def pack_kernel(first_ref, held_ref, out_ref, sem):
+def pack_kernel(first_ref, held_ref, out_ref):
     slots = held_ref.shape[0]
     domains, per_peer = out_ref.shape[:2]
-    for d in range(domains):
+
+    def one(d, carry):
         for t in range(per_peer):
-            slot = jnp.minimum(first_ref[d] + t, slots - 1)
-            pltpu.make_async_copy(held_ref.at[slot], out_ref.at[d, t], sem).start()
-    pltpu.make_async_copy(out_ref, out_ref, sem).wait()
+            out_ref[d, t] = held_ref[jnp.minimum(first_ref[d] + t, slots - 1)]
+        return carry
+
+    lax.fori_loop(0, domains, one, 0)
 
 
 def pack(first_slot, held, per_peer):
     return pl.pallas_call(
         pack_kernel,
         out_shape=jax.ShapeDtypeStruct((first_slot.shape[0], per_peer) + held.shape[1:], held.dtype),
-        grid_spec=pltpu.PrefetchScalarGridSpec(
-            num_scalar_prefetch=1,
-            grid=(1,),
-            in_specs=[pl.BlockSpec(memory_space=pl.ANY)],
-            out_specs=pl.BlockSpec(memory_space=pl.ANY),
-            scratch_shapes=[pltpu.SemaphoreType.DMA],
-        ),
+        in_specs=[pl.BlockSpec(memory_space=pltpu.SMEM), pl.BlockSpec(memory_space=pltpu.VMEM)],
+        out_specs=pl.BlockSpec(memory_space=pltpu.VMEM),
+        compiler_params=pltpu.CompilerParams(vmem_limit_bytes=24 * 1024 * 1024),
         name="pack",
     )(first_slot, held)
 
 
 def step_kernel(mode, base, extras, meta_ref, pattern_ref, coeffs_ref, *refs):
     pieces, refs = refs[:9], refs[9:]
-    overflow, refs = refs[:extras], refs[extras:]
+    overflow, refs = refs[: 3 * extras], refs[3 * extras :]
     blocks_ref, refs = refs[0], refs[1:]
     halo, acc, sems = refs[-3:]
     refs = refs[:-3]
@@ -50,22 +48,30 @@
         size = pieces[c].shape[0]
         return pltpu.make_async_copy(pieces[c], halo.at[pl.ds(c * capacity, size)], sems.at[c])
 
-    def extra_copy(h):
+    def extra_copy(h, column):
         code = meta_ref[1 + h]
         return pltpu.make_async_copy(
-            overflow[h], halo.at[pl.ds(code * capacity + base, capacity - base)], sems.at[9 + h]
+            overflow[3 * h + column],
+            halo.at[pl.ds(code * capacity + base, capacity - base)],
+            sems.at[9 + h],
         )
+
+    def each_extra(act):
+        for h in range(extras):
+            for column in range(3):
+                code = meta_ref[1 + h]
+                pl.when((code >= 0) & (lax.rem(code, 3) == column))(
+                    lambda h=h, column=column: act(extra_copy(h, column))
+                )
 
     @pl.when(r == 0)
     def _():
         for c in range(9):
             piece_copy(c).start()
-        for h in range(extras):
-            pl.when(meta_ref[1 + h] >= 0)(lambda h=h: extra_copy(h).start())
+        each_extra(lambda copy: copy.start())
         for c in range(9):
             piece_copy(c).wait()
-        for h in range(extras):
-            pl.when(meta_ref[1 + h] >= 0)(lambda h=h: extra_copy(h).wait())
+        each_extra(lambda copy: copy.wait())
 
     @pl.when(r < count)
     def _():
@@ -117,7 +123,7 @@
     narrow = jax.ShapeDtypeStruct(shape, jnp.bfloat16)
     outs = [wide] if mode == 3 else [narrow, wide]
     return pl.pallas_call(
-        functools.partial(step_kernel, mode, base, len(overflow)),
+        functools.partial(step_kernel, mode, base, len(overflow) // 3),
         out_shape=outs,
         grid_spec=pltpu.PrefetchScalarGridSpec(
             num_scalar_prefetch=2,
@@ -187,13 +193,15 @@
         meta = jnp.stack(meta).astype(jnp.int32)
 
         def run(mode, panels, *rest):
-            overflow = [
-                lax.psum(
-                    jnp.where(d == my_domain, panels[base:], jnp.zeros((), panels.dtype)), ("gx", "gy")
-                )
-                for d in heavy
-            ]
             pieces = halo_pieces(panels, base)
+            overflow = []
+            if heavy:
+                own = panels[base:]
+                above, below = shifted(own, "gx", 1), shifted(own, "gx", -1)
+            for d in heavy:
+                row = (d // grid_cols - my_row + 1) % grid_rows
+                middle = jnp.where(row == 0, above, jnp.where(row == 1, own, below))
+                overflow += [shifted(middle, "gy", 1), middle, shifted(middle, "gy", -1)]
             return step(mode, base, meta, table, coeffs, pieces, overflow, rows, rest)
 
         sent, one = run(1, start)

time: 753 us -> 426 us (0.57)
  the two profiles are of different devices: /device:TPU:1 before, /device:TPU:0 now
where the time goes in v2:
time: 426 us; the launch traced here: 429 us
  waiting for transfers between devices  283 us (66%)
  starting transfers between devices  83.7 us (20%)
  Pallas kernels  33.7 us (8%)
  local copies, waits for them, and re-layouts  17.2 us (4%)
  other arithmetic  5.24 us (1%)
    ppermute x36, waiting for transfers between devices, shifted(): return lax.ppermute(x, axis, [(i, (i + by) % count) for i in range(count)])  248 us
    ppermute x36, starting transfers between devices, shifted(): return lax.ppermute(x, axis, [(i, (i + by) % count) for i in range(count)])  76.4 us
    all_to_all x1, waiting for transfers between devices, local(): lax.all_to_all(outgoing, ('gx', 'gy'), split_axis=0, concat_axis=3, tiled...  35.3 us
    pallas_call x3, Pallas kernels, step(): pl.pallas_call(functools.partial(step_kernel, mode, base, len(overflow) /...  32.3 us
  transfers between devices with their start and end apart: 37, of which 14 were waited for; matrix products, arithmetic and copies ran while one was open for 1% of the time, Pallas kernels for 0%

profile of v2, /device:TPU:0, one launch (start us, length us, event | category | flops | bytes accessed | tf_op | source)
XLA Modules:
  0.0 429.5 jit_solution(10047232487082717990)
XLA Ops:
  12.0 7.3 %all-to-all-start = ((bf16[32,3,128,64]{2,3,1,0:T(8,128)(2,1)}), bf16[32,3,128,64]{2,3,1,0:T(8,128)(2,1)S(1)}, u32[]{:S(2)}, u32[]{:S(2)}) async-start(bf16[32,3,128,64]{2,3,1,0:T(8,128)(2,1)} %copy.15), calls=%async_computation | async-start | bytes 3145728 | tf_op jit(solution)/shard_map/all_to_all | solution.py:179
  21.8 35.3 %all-to-all-done = bf16[32,3,128,64]{2,3,1,0:T(8,128)(2,1)S(1)} async-done(((bf16[32,3,128,64]{2,3,1,0:T(8,128)(2,1)}), bf16[32,3,128,64]{2,3,1,0:T(8,128)(2,1)S(1)}, u32[]{:S(2)}, u32[]{:S(2)}) %all-to-all-start) | async-done | bytes 1572896 | tf_op jit(solution)/shard_map/all_to_all | solution.py:179
  59.5 370.0 %conditional.1 = (f32[1,1,12,128,512]{4,3,2,1,0:T(8,128)}) conditional(s32[]{:T(128)} %convert_element_type.10, (s32[]{:T(128)}, bf16[12,128,512]{2,1,0:T(8,128)(2,1)}, s32[12,24]{1,0:T(8,128)S(1)}, f32[4]{0:T(128)S(1)}, bf16[12,24,128,128]{3,2,1,0:T(8,128)(2,1)}) %tuple.30, (s32[]{:T(128)}, s32[32,32]{1,0:T(8,128)S(1)}, s32[32]{0:T(128)S(1)}, ...), branch_computations={%region_4.5_spmd, %region_5.8_spmd} | conditional | flops 1967258 | bytes 185598944 | solution.py:217
  69.5 22.9 %collective-permute-done.33 = bf16[5,128,512]{2,1,0:T(8,128)(2,1)S(1)} collective-permute-done((bf16[5,128,512]{2,1,0:T(8,128)(2,1)S(1)}, bf16[5,128,512]{2,1,0:T(8,128)(2,1)S(1)}, u32[]{:S(2)}, u32[]{:S(2)}) %collective-permute-start.33) | collective-permute-done | bytes 655392 | tf_op jit(solution)/shard_map/cond/branch_1_fun/ppermute | solution.py:149
  100.6 10.5 %collective-permute-done.29.refs_7_ = bf16[7,128,512]{2,1,0:T(8,128)(2,1)S(1)} collective-permute-done((bf16[7,128,512]{2,1,0:T(8,128)(2,1)}, bf16[7,128,512]{2,1,0:T(8,128)(2,1)S(1)}, u32[]{:S(2)}, u32[]{:S(2)}) %collective-permute-start.29) | collective-permute-done | bytes 917536 | tf_op jit(solution)/shard_map/cond/branch_1_fun/ppermute | solution.py:149
  111.6 19.4 %collective-permute-done.24.refs_1_ = bf16[7,128,512]{2,1,0:T(8,128)(2,1)S(1)} collective-permute-done((bf16[7,128,512]{2,1,0:T(8,128)(2,1)}, bf16[7,128,512]{2,1,0:T(8,128)(2,1)S(1)}, u32[]{:S(2)}, u32[]{:S(2)}) %collective-permute-start.24) | collective-permute-done | bytes 917536 | tf_op jit(solution)/shard_map/cond/branch_1_fun/ppermute | solution.py:149
  136.2 25.4 %collective-permute-done.34.refs_9_ = bf16[5,128,512]{2,1,0:T(8,128)(2,1)} collective-permute-done((bf16[5,128,512]{2,1,0:T(8,128)(2,1)S(1)}, bf16[5,128,512]{2,1,0:T(8,128)(2,1)}, u32[]{:S(2)}, u32[]{:S(2)}) %collective-permute-start.34) | collective-permute-done | bytes 655392 | tf_op jit(solution)/shard_map/cond/branch_1_fun/ppermute | solution.py:149
  162.7 9.5 %step1.3 = (bf16[12,128,512]{2,1,0:T(8,128)(2,1)S(1)}, f32[12,128,512]{2,1,0:T(8,128)S(1)}) custom-call(s32[2]{0:T(128)S(1)} %pad_add_fusion.meta_ref, s32[12,24]{1,0:T(8,128)S(1)} %get-tuple-element.70.pattern_ref, f32[4]{0:T(128)S(1)} %get-tuple-element.71.coeffs_ref, bf16[7,128,512]{2,1,0:T(8,128)(2,1)} %collective-permute-done.25.refs_0_, ...), custom_call_target="tpu_custom_call" | custom-call | tf_op jit(solution)/shard_map/cond/branch_1_fun/step1/pallas_call | solution.py:125
  172.3 5.9 %collective-permute-start.45 = (bf16[5,128,512]{2,1,0:T(8,128)(2,1)S(1)}, bf16[5,128,512]{2,1,0:T(8,128)(2,1)S(1)}, u32[]{:S(2)}, u32[]{:S(2)}) collective-permute-start(bf16[5,128,512]{2,1,0:T(8,128)(2,1)S(1)} %slice.15), channel_id=1, source_target_pairs={{0,24},{8,0},{16,8},{24,16},{1,25},{9,1},{17,9},{25,17},{2,26},{10... | collective-permute-start | bytes 1966088 | tf_op jit(solution)/shard_map/cond/branch_1_fun/ppermute | solution.py:149
  182.1 8.7 %collective-permute-done.45 = bf16[5,128,512]{2,1,0:T(8,128)(2,1)S(1)} collective-permute-done((bf16[5,128,512]{2,1,0:T(8,128)(2,1)S(1)}, bf16[5,128,512]{2,1,0:T(8,128)(2,1)S(1)}, u32[]{:S(2)}, u32[]{:S(2)}) %collective-permute-start.45) | collective-permute-done | bytes 655392 | tf_op jit(solution)/shard_map/cond/branch_1_fun/ppermute | solution.py:149
  190.8 21.4 %collective-permute-start.39 = (bf16[7,128,512]{2,1,0:T(8,128)(2,1)S(1)}, bf16[7,128,512]{2,1,0:T(8,128)(2,1)S(1)}, u32[]{:S(2)}, u32[]{:S(2)}) collective-permute-start(bf16[7,128,512]{2,1,0:T(8,128)(2,1)S(1)} %slice.14), channel_id=1, source_target_pairs={{0,1},{1,2},{2,3},{3,4},{4,5},{5,6},{6,7},{7,0},{8,9},{9,10},{10,1... | collective-permute-start | bytes 2752520 | tf_op jit(solution)/shard_map/cond/branch_1_fun/ppermute | solution.py:149
  212.4 12.1 %collective-permute-done.41.refs_7_ = bf16[7,128,512]{2,1,0:T(8,128)(2,1)S(1)} collective-permute-done((bf16[7,128,512]{2,1,0:T(8,128)(2,1)S(1)}, bf16[7,128,512]{2,1,0:T(8,128)(2,1)S(1)}, u32[]{:S(2)}, u32[]{:S(2)}) %collective-permute-start.41) | collective-permute-done | bytes 917536 | tf_op jit(solution)/shard_map/cond/branch_1_fun/ppermute | solution.py:149
  224.5 5.2 %collective-permute-start.42 = (bf16[7,128,512]{2,1,0:T(8,128)(2,1)S(1)}, bf16[7,128,512]{2,1,0:T(8,128)(2,1)S(1)}, u32[]{:S(2)}, u32[]{:S(2)}) collective-permute-start(bf16[7,128,512]{2,1,0:T(8,128)(2,1)S(1)} %collective-permute-done.41.refs_7_), channel_id=1, source_target_pairs={{0,1},{1,2},{2,3},{3,4},{4,5},{5,6},{6,7},{7,0},{8,9},{9,10},{10,1... | collective-permute-start | bytes 2752520 | tf_op jit(solution)/shard_map/cond/branch_1_fun/ppermute | solution.py:149
  229.7 17.0 %collective-permute-done.36.refs_1_ = bf16[7,128,512]{2,1,0:T(8,128)(2,1)S(1)} collective-permute-done((bf16[7,128,512]{2,1,0:T(8,128)(2,1)S(1)}, bf16[7,128,512]{2,1,0:T(8,128)(2,1)S(1)}, u32[]{:S(2)}, u32[]{:S(2)}) %collective-permute-start.36) | collective-permute-done | bytes 917536 | tf_op jit(solution)/shard_map/cond/branch_1_fun/ppermute | solution.py:149
  247.3 6.3 %collective-permute-start.46 = (bf16[5,128,512]{2,1,0:T(8,128)(2,1)S(1)}, bf16[5,128,512]{2,1,0:T(8,128)(2,1)S(1)}, u32[]{:S(2)}, u32[]{:S(2)}) collective-permute-start(bf16[5,128,512]{2,1,0:T(8,128)(2,1)S(1)} %select_select_fusion.1.refs_10_), channel_id=1, source_target_pairs={{0,1},{1,2},{2,3},{3,4},{4,5},{5,6},{6,7},{7,0},{8,9},{9,10},{10,1... | collective-permute-start | bytes 1966088 | tf_op jit(solution)/shard_map/cond/branch_1_fun/ppermute | solution.py:149
  253.6 34.4 %collective-permute-done.46.refs_9_ = bf16[5,128,512]{2,1,0:T(8,128)(2,1)S(1)} collective-permute-done((bf16[5,128,512]{2,1,0:T(8,128)(2,1)S(1)}, bf16[5,128,512]{2,1,0:T(8,128)(2,1)S(1)}, u32[]{:S(2)}, u32[]{:S(2)}) %collective-permute-start.46) | collective-permute-done | bytes 655392 | tf_op jit(solution)/shard_map/cond/branch_1_fun/ppermute | solution.py:149
  288.0 11.6 %step2.3 = (bf16[12,128,512]{2,1,0:T(8,128)(2,1)S(1)}, f32[12,128,512]{2,1,0:T(8,128)}) custom-call(s32[2]{0:T(128)S(1)} %pad_add_fusion.meta_ref, s32[12,24]{1,0:T(8,128)S(1)} %get-tuple-element.70.pattern_ref, f32[4]{0:T(128)S(1)} %get-tuple-element.71.coeffs_ref, bf16[7,128,512]{2,1,0:T(8,128)(2,1)S(1)} %collective-permute-done.37.refs_0_, ...), custom_call_target="tpu_custom_call" | custom-call | tf_op jit(solution)/shard_map/cond/branch_1_fun/step2/pallas_call | solution.py:125
  306.1 15.2 %collective-permute-done.57 = bf16[5,128,512]{2,1,0:T(8,128)(2,1)S(1)} collective-permute-done((bf16[5,128,512]{2,1,0:T(8,128)(2,1)S(1)}, bf16[5,128,512]{2,1,0:T(8,128)(2,1)S(1)}, u32[]{:S(2)}, u32[]{:S(2)}) %collective-permute-start.57) | collective-permute-done | bytes 655392 | tf_op jit(solution)/shard_map/cond/branch_1_fun/ppermute | solution.py:149
  321.3 10.5 %collective-permute-done.56 = bf16[5,128,512]{2,1,0:T(8,128)(2,1)S(1)} collective-permute-done((bf16[5,128,512]{2,1,0:T(8,128)(2,1)S(1)}, bf16[5,128,512]{2,1,0:T(8,128)(2,1)S(1)}, u32[]{:S(2)}, u32[]{:S(2)}) %collective-permute-start.56) | collective-permute-done | bytes 655392 | tf_op jit(solution)/shard_map/cond/branch_1_fun/ppermute | solution.py:149
  332.0 15.2 %collective-permute-done.53.refs_7_ = bf16[7,128,512]{2,1,0:T(8,128)(2,1)S(1)} collective-permute-done((bf16[7,128,512]{2,1,0:T(8,128)(2,1)S(1)}, bf16[7,128,512]{2,1,0:T(8,128)(2,1)S(1)}, u32[]{:S(2)}, u32[]{:S(2)}) %collective-permute-start.53) | collective-permute-done | bytes 917536 | tf_op jit(solution)/shard_map/cond/branch_1_fun/ppermute | solution.py:149
  348.8 8.9 %collective-permute-done.48.refs_1_ = bf16[7,128,512]{2,1,0:T(8,128)(2,1)S(1)} collective-permute-done((bf16[7,128,512]{2,1,0:T(8,128)(2,1)S(1)}, bf16[7,128,512]{2,1,0:T(8,128)(2,1)S(1)}, u32[]{:S(2)}, u32[]{:S(2)}) %collective-permute-start.48) | collective-permute-done | bytes 917536 | tf_op jit(solution)/shard_map/cond/branch_1_fun/ppermute | solution.py:149
  357.7 12.9 %collective-permute-start.50 = (bf16[7,128,512]{2,1,0:T(8,128)(2,1)S(1)}, bf16[7,128,512]{2,1,0:T(8,128)(2,1)S(1)}, u32[]{:S(2)}, u32[]{:S(2)}) collective-permute-start(bf16[7,128,512]{2,1,0:T(8,128)(2,1)S(1)} %collective-permute-done.48.refs_1_), channel_id=1, source_target_pairs={{0,7},{1,0},{2,1},{3,2},{4,3},{5,4},{6,5},{7,6},{8,15},{9,8},{10,9... | collective-permute-start | bytes 2752520 | tf_op jit(solution)/shard_map/cond/branch_1_fun/ppermute | solution.py:149
  370.7 47.5 %collective-permute-done.58.refs_9_ = bf16[5,128,512]{2,1,0:T(8,128)(2,1)S(1)} collective-permute-done((bf16[5,128,512]{2,1,0:T(8,128)(2,1)S(1)}, bf16[5,128,512]{2,1,0:T(8,128)(2,1)S(1)}, u32[]{:S(2)}, u32[]{:S(2)}) %collective-permute-start.58) | collective-permute-done | bytes 655392 | tf_op jit(solution)/shard_map/cond/branch_1_fun/ppermute | solution.py:149
  418.3 11.2 %step3.3 = f32[12,128,512]{2,1,0:T(8,128)} custom-call(s32[2]{0:T(128)S(1)} %pad_add_fusion.meta_ref, s32[12,24]{1,0:T(8,128)S(1)} %get-tuple-element.70.pattern_ref, f32[4]{0:T(128)S(1)} %get-tuple-element.71.coeffs_ref, bf16[7,128,512]{2,1,0:T(8,128)(2,1)S(1)} %collective-permute-done.49.refs_0_, bf16[7,128,512]{2,1,0:T(8,128)(2,1)S(1)} %collective-permute-done.48.refs_1_, ...), custom_call_target="tpu_custom_call" | custom-call | tf_op jit(solution)/shard_map/cond/branch_1_fun/step3/pallas_call | solution.py:125
  (101 shorter events, 48.7 us)
Async XLA Ops:
  12.0 45.0 %all-to-all-start = ((bf16[32,3,128,64]{2,3,1,0:T(8,128)(2,1)}), bf16[32,3,128,64]{2,3,1,0:T(8,128)(2,1)S(1)}, u32[]{:S(2)}, u32[]{:S(2)}) async-start(bf16[32,3,128,64]{2,3,1,0:T(8,128)(2,1)} %copy.15), calls=%async_computation | async-start | bytes 3145728 | tf_op jit(solution)/shard_map/all_to_all | solution.py:179
  64.9 46.2 %collective-permute-start.29 = (bf16[7,128,512]{2,1,0:T(8,128)(2,1)}, bf16[7,128,512]{2,1,0:T(8,128)(2,1)S(1)}, u32[]{:S(2)}, u32[]{:S(2)}) collective-permute-start(bf16[7,128,512]{2,1,0:T(8,128)(2,1)} %slice.12), channel_id=1, source_target_pairs={{0,24},{8,0},{16,8},{24,16},{1,25},{9,1},{17,9},{25,17},{2,26},{10... | collective-permute-start | bytes 2752520 | tf_op jit(solution)/shard_map/cond/branch_1_fun/ppermute | solution.py:149
  68.1 43.5 %collective-permute-start.28 = (bf16[7,128,512]{2,1,0:T(8,128)(2,1)}, bf16[7,128,512]{2,1,0:T(8,128)(2,1)S(1)}, u32[]{:S(2)}, u32[]{:S(2)}) collective-permute-start(bf16[7,128,512]{2,1,0:T(8,128)(2,1)} %slice.12), channel_id=1, source_target_pairs={{0,7},{1,0},{2,1},{3,2},{4,3},{5,4},{6,5},{7,6},{8,15},{9,8},{10,9... | collective-permute-start | bytes 2752520 | tf_op jit(solution)/shard_map/cond/branch_1_fun/ppermute | solution.py:149
  69.5 61.5 %collective-permute-start.24 = (bf16[7,128,512]{2,1,0:T(8,128)(2,1)}, bf16[7,128,512]{2,1,0:T(8,128)(2,1)S(1)}, u32[]{:S(2)}, u32[]{:S(2)}) collective-permute-start(bf16[7,128,512]{2,1,0:T(8,128)(2,1)} %slice.12), channel_id=1, source_target_pairs={{0,8},{8,16},{16,24},{24,0},{1,9},{9,17},{17,25},{25,1},{2,10},{10... | collective-permute-start | bytes 2752520 | tf_op jit(solution)/shard_map/cond/branch_1_fun/ppermute | solution.py:149
  111.1 50.5 %collective-permute-start.31 = (bf16[7,128,512]{2,1,0:T(8,128)(2,1)S(1)}, bf16[7,128,512]{2,1,0:T(8,128)(2,1)}, u32[]{:S(2)}, u32[]{:S(2)}) collective-permute-start(bf16[7,128,512]{2,1,0:T(8,128)(2,1)S(1)} %collective-permute-done.29.refs_7_), channel_id=1, source_target_pairs={{0,7},{1,0},{2,1},{3,2},{4,3},{5,4},{6,5},{7,6},{8,15},{9,8},{10,9... | collective-permute-start | bytes 2752520 | tf_op jit(solution)/shard_map/cond/branch_1_fun/ppermute | solution.py:149
  111.6 50.0 %collective-permute-start.30 = (bf16[7,128,512]{2,1,0:T(8,128)(2,1)S(1)}, bf16[7,128,512]{2,1,0:T(8,128)(2,1)}, u32[]{:S(2)}, u32[]{:S(2)}) collective-permute-start(bf16[7,128,512]{2,1,0:T(8,128)(2,1)S(1)} %collective-permute-done.29.refs_7_), channel_id=1, source_target_pairs={{0,1},{1,2},{2,3},{3,4},{4,5},{5,6},{6,7},{7,0},{8,9},{9,10},{10,1... | collective-permute-start | bytes 2752520 | tf_op jit(solution)/shard_map/cond/branch_1_fun/ppermute | solution.py:149
  178.2 46.3 %collective-permute-start.41 = (bf16[7,128,512]{2,1,0:T(8,128)(2,1)S(1)}, bf16[7,128,512]{2,1,0:T(8,128)(2,1)S(1)}, u32[]{:S(2)}, u32[]{:S(2)}) collective-permute-start(bf16[7,128,512]{2,1,0:T(8,128)(2,1)S(1)} %slice.14), channel_id=1, source_target_pairs={{0,24},{8,0},{16,8},{24,16},{1,25},{9,1},{17,9},{25,17},{2,26},{10... | collective-permute-start | bytes 2752520 | tf_op jit(solution)/shard_map/cond/branch_1_fun/ppermute | solution.py:149
  182.1 42.4 %collective-permute-start.40 = (bf16[7,128,512]{2,1,0:T(8,128)(2,1)S(1)}, bf16[7,128,512]{2,1,0:T(8,128)(2,1)S(1)}, u32[]{:S(2)}, u32[]{:S(2)}) collective-permute-start(bf16[7,128,512]{2,1,0:T(8,128)(2,1)S(1)} %slice.14), channel_id=1, source_target_pairs={{0,7},{1,0},{2,1},{3,2},{4,3},{5,4},{6,5},{7,6},{8,15},{9,8},{10,9... | collective-permute-start | bytes 2752520 | tf_op jit(solution)/shard_map/cond/branch_1_fun/ppermute | solution.py:149
  182.1 64.7 %collective-permute-start.36 = (bf16[7,128,512]{2,1,0:T(8,128)(2,1)S(1)}, bf16[7,128,512]{2,1,0:T(8,128)(2,1)S(1)}, u32[]{:S(2)}, u32[]{:S(2)}) collective-permute-start(bf16[7,128,512]{2,1,0:T(8,128)(2,1)S(1)} %slice.14), channel_id=1, source_target_pairs={{0,8},{8,16},{16,24},{24,0},{1,9},{9,17},{17,25},{25,1},{2,10},{10... | collective-permute-start | bytes 2752520 | tf_op jit(solution)/shard_map/cond/branch_1_fun/ppermute | solution.py:149
  190.8 56.0 %collective-permute-start.39 = (bf16[7,128,512]{2,1,0:T(8,128)(2,1)S(1)}, bf16[7,128,512]{2,1,0:T(8,128)(2,1)S(1)}, u32[]{:S(2)}, u32[]{:S(2)}) collective-permute-start(bf16[7,128,512]{2,1,0:T(8,128)(2,1)S(1)} %slice.14), channel_id=1, source_target_pairs={{0,1},{1,2},{2,3},{3,4},{4,5},{5,6},{6,7},{7,0},{8,9},{9,10},{10,1... | collective-permute-start | bytes 2752520 | tf_op jit(solution)/shard_map/cond/branch_1_fun/ppermute | solution.py:149
  224.5 63.4 %collective-permute-start.43 = (bf16[7,128,512]{2,1,0:T(8,128)(2,1)S(1)}, bf16[7,128,512]{2,1,0:T(8,128)(2,1)S(1)}, u32[]{:S(2)}, u32[]{:S(2)}) collective-permute-start(bf16[7,128,512]{2,1,0:T(8,128)(2,1)S(1)} %collective-permute-done.41.refs_7_), channel_id=1, source_target_pairs={{0,7},{1,0},{2,1},{3,2},{4,3},{5,4},{6,5},{7,6},{8,15},{9,8},{10,9... | collective-permute-start | bytes 2752520 | tf_op jit(solution)/shard_map/cond/branch_1_fun/ppermute | solution.py:149
  224.5 63.4 %collective-permute-start.42 = (bf16[7,128,512]{2,1,0:T(8,128)(2,1)S(1)}, bf16[7,128,512]{2,1,0:T(8,128)(2,1)S(1)}, u32[]{:S(2)}, u32[]{:S(2)}) collective-permute-start(bf16[7,128,512]{2,1,0:T(8,128)(2,1)S(1)} %collective-permute-done.41.refs_7_), channel_id=1, source_target_pairs={{0,1},{1,2},{2,3},{3,4},{4,5},{5,6},{6,7},{7,0},{8,9},{9,10},{10,1... | collective-permute-start | bytes 2752520 | tf_op jit(solution)/shard_map/cond/branch_1_fun/ppermute | solution.py:149
  246.8 41.2 %collective-permute-start.38 = (bf16[7,128,512]{2,1,0:T(8,128)(2,1)S(1)}, bf16[7,128,512]{2,1,0:T(8,128)(2,1)S(1)}, u32[]{:S(2)}, u32[]{:S(2)}) collective-permute-start(bf16[7,128,512]{2,1,0:T(8,128)(2,1)S(1)} %collective-permute-done.36.refs_1_), channel_id=1, source_target_pairs={{0,7},{1,0},{2,1},{3,2},{4,3},{5,4},{6,5},{7,6},{8,15},{9,8},{10,9... | collective-permute-start | bytes 2752520 | tf_op jit(solution)/shard_map/cond/branch_1_fun/ppermute | solution.py:149
  246.8 41.2 %collective-permute-start.37 = (bf16[7,128,512]{2,1,0:T(8,128)(2,1)S(1)}, bf16[7,128,512]{2,1,0:T(8,128)(2,1)S(1)}, u32[]{:S(2)}, u32[]{:S(2)}) collective-permute-start(bf16[7,128,512]{2,1,0:T(8,128)(2,1)S(1)} %collective-permute-done.36.refs_1_), channel_id=1, source_target_pairs={{0,1},{1,2},{2,3},{3,4},{4,5},{5,6},{6,7},{7,0},{8,9},{9,10},{10,1... | collective-permute-start | bytes 2752520 | tf_op jit(solution)/shard_map/cond/branch_1_fun/ppermute | solution.py:149
  247.3 40.7 %collective-permute-start.46 = (bf16[5,128,512]{2,1,0:T(8,128)(2,1)S(1)}, bf16[5,128,512]{2,1,0:T(8,128)(2,1)S(1)}, u32[]{:S(2)}, u32[]{:S(2)}) collective-permute-start(bf16[5,128,512]{2,1,0:T(8,128)(2,1)S(1)} %select_select_fusion.1.refs_10_), channel_id=1, source_target_pairs={{0,1},{1,2},{2,3},{3,4},{4,5},{5,6},{6,7},{7,0},{8,9},{9,10},{10,1... | collective-permute-start | bytes 1966088 | tf_op jit(solution)/shard_map/cond/branch_1_fun/ppermute | solution.py:149
  303.9 43.3 %collective-permute-start.53 = (bf16[7,128,512]{2,1,0:T(8,128)(2,1)S(1)}, bf16[7,128,512]{2,1,0:T(8,128)(2,1)S(1)}, u32[]{:S(2)}, u32[]{:S(2)}) collective-permute-start(bf16[7,128,512]{2,1,0:T(8,128)(2,1)S(1)} %slice.16), channel_id=1, source_target_pairs={{0,24},{8,0},{16,8},{24,16},{1,25},{9,1},{17,9},{25,17},{2,26},{10... | collective-permute-start | bytes 2752520 | tf_op jit(solution)/shard_map/cond/branch_1_fun/ppermute | solution.py:149
  304.0 44.8 %collective-permute-start.52 = (bf16[7,128,512]{2,1,0:T(8,128)(2,1)S(1)}, bf16[7,128,512]{2,1,0:T(8,128)(2,1)S(1)}, u32[]{:S(2)}, u32[]{:S(2)}) collective-permute-start(bf16[7,128,512]{2,1,0:T(8,128)(2,1)S(1)} %slice.16), channel_id=1, source_target_pairs={{0,7},{1,0},{2,1},{3,2},{4,3},{5,4},{6,5},{7,6},{8,15},{9,8},{10,9... | collective-permute-start | bytes 2752520 | tf_op jit(solution)/shard_map/cond/branch_1_fun/ppermute | solution.py:149
  304.1 53.7 %collective-permute-start.48 = (bf16[7,128,512]{2,1,0:T(8,128)(2,1)S(1)}, bf16[7,128,512]{2,1,0:T(8,128)(2,1)S(1)}, u32[]{:S(2)}, u32[]{:S(2)}) collective-permute-start(bf16[7,128,512]{2,1,0:T(8,128)(2,1)S(1)} %slice.16), channel_id=1, source_target_pairs={{0,8},{8,16},{16,24},{24,0},{1,9},{9,17},{17,25},{25,1},{2,10},{10... | collective-permute-start | bytes 2752520 | tf_op jit(solution)/shard_map/cond/branch_1_fun/ppermute | solution.py:149
  321.3 49.4 %collective-permute-start.51 = (bf16[7,128,512]{2,1,0:T(8,128)(2,1)S(1)}, bf16[7,128,512]{2,1,0:T(8,128)(2,1)S(1)}, u32[]{:S(2)}, u32[]{:S(2)}) collective-permute-start(bf16[7,128,512]{2,1,0:T(8,128)(2,1)S(1)} %slice.16), channel_id=1, source_target_pairs={{0,1},{1,2},{2,3},{3,4},{4,5},{5,6},{6,7},{7,0},{8,9},{9,10},{10,1... | collective-permute-start | bytes 2752520 | tf_op jit(solution)/shard_map/cond/branch_1_fun/ppermute | solution.py:149
  347.2 71.0 %collective-permute-start.55 = (bf16[7,128,512]{2,1,0:T(8,128)(2,1)S(1)}, bf16[7,128,512]{2,1,0:T(8,128)(2,1)S(1)}, u32[]{:S(2)}, u32[]{:S(2)}) collective-permute-start(bf16[7,128,512]{2,1,0:T(8,128)(2,1)S(1)} %collective-permute-done.53.refs_7_), channel_id=1, source_target_pairs={{0,7},{1,0},{2,1},{3,2},{4,3},{5,4},{6,5},{7,6},{8,15},{9,8},{10,9... | collective-permute-start | bytes 2752520 | tf_op jit(solution)/shard_map/cond/branch_1_fun/ppermute | solution.py:149
  348.8 69.4 %collective-permute-start.54 = (bf16[7,128,512]{2,1,0:T(8,128)(2,1)S(1)}, bf16[7,128,512]{2,1,0:T(8,128)(2,1)S(1)}, u32[]{:S(2)}, u32[]{:S(2)}) collective-permute-start(bf16[7,128,512]{2,1,0:T(8,128)(2,1)S(1)} %collective-permute-done.53.refs_7_), channel_id=1, source_target_pairs={{0,1},{1,2},{2,3},{3,4},{4,5},{5,6},{6,7},{7,0},{8,9},{9,10},{10,1... | collective-permute-start | bytes 2752520 | tf_op jit(solution)/shard_map/cond/branch_1_fun/ppermute | solution.py:149
  357.7 60.5 %collective-permute-start.50 = (bf16[7,128,512]{2,1,0:T(8,128)(2,1)S(1)}, bf16[7,128,512]{2,1,0:T(8,128)(2,1)S(1)}, u32[]{:S(2)}, u32[]{:S(2)}) collective-permute-start(bf16[7,128,512]{2,1,0:T(8,128)(2,1)S(1)} %collective-permute-done.48.refs_1_), channel_id=1, source_target_pairs={{0,7},{1,0},{2,1},{3,2},{4,3},{5,4},{6,5},{7,6},{8,15},{9,8},{10,9... | collective-permute-start | bytes 2752520 | tf_op jit(solution)/shard_map/cond/branch_1_fun/ppermute | solution.py:149
  370.7 47.5 %collective-permute-start.49 = (bf16[7,128,512]{2,1,0:T(8,128)(2,1)S(1)}, bf16[7,128,512]{2,1,0:T(8,128)(2,1)S(1)}, u32[]{:S(2)}, u32[]{:S(2)}) collective-permute-start(bf16[7,128,512]{2,1,0:T(8,128)(2,1)S(1)} %collective-permute-done.48.refs_1_), channel_id=1, source_target_pairs={{0,1},{1,2},{2,3},{3,4},{4,5},{5,6},{6,7},{7,0},{8,9},{9,10},{10,1... | collective-permute-start | bytes 2752520 | tf_op jit(solution)/shard_map/cond/branch_1_fun/ppermute | solution.py:149
  370.7 47.5 %collective-permute-start.58 = (bf16[5,128,512]{2,1,0:T(8,128)(2,1)S(1)}, bf16[5,128,512]{2,1,0:T(8,128)(2,1)S(1)}, u32[]{:S(2)}, u32[]{:S(2)}) collective-permute-start(bf16[5,128,512]{2,1,0:T(8,128)(2,1)S(1)} %select_select_fusion.refs_10_), channel_id=1, source_target_pairs={{0,1},{1,2},{2,3},{3,4},{4,5},{5,6},{6,7},{7,0},{8,9},{9,10},{10,1... | collective-permute-start | bytes 1966088 | tf_op jit(solution)/shard_map/cond/branch_1_fun/ppermute | solution.py:149
  (23 other events, 1045.0 us)

commit v3 on v2

--- a/solution.py
+++ b/solution.py
@@ -35,8 +35,9 @@
 
 
 def step_kernel(mode, base, extras, meta_ref, pattern_ref, coeffs_ref, *refs):
-    pieces, refs = refs[:9], refs[9:]
-    overflow, refs = refs[: 3 * extras], refs[3 * extras :]
+    panels_ref, ring_ref, refs = refs[0], refs[1], refs[2:]
+    if extras:
+        extra_ref, refs = refs[0], refs[1:]
     blocks_ref, refs = refs[0], refs[1:]
     halo, acc, sems = refs[-3:]
     refs = refs[:-3]
@@ -45,13 +46,15 @@
     capacity, slots = pattern_ref.shape
 
     def piece_copy(c):
-        size = pieces[c].shape[0]
-        return pltpu.make_async_copy(pieces[c], halo.at[pl.ds(c * capacity, size)], sems.at[c])
+        source = panels_ref if c == OWN else ring_ref.at[c]
+        return pltpu.make_async_copy(
+            source, halo.at[pl.ds(c * capacity, source.shape[0])], sems.at[c]
+        )
 
     def extra_copy(h, column):
         code = meta_ref[1 + h]
         return pltpu.make_async_copy(
-            overflow[3 * h + column],
+            extra_ref.at[h, column],
             halo.at[pl.ds(code * capacity + base, capacity - base)],
             sems.at[9 + h],
         )
@@ -109,9 +112,10 @@
             ref[...] = jnp.zeros_like(ref)
 
 
-def step(mode, base, meta, pattern, coeffs, pieces, overflow, blocks, panels):
+def step(mode, base, meta, pattern, coeffs, pieces, blocks, panels):
     capacity, slots = pattern.shape
     rows, cols = pieces[0].shape[1:]
+    extras = meta.shape[0] - 1
 
     def live(r, meta, pattern):
         return jnp.minimum(r, meta[0] - 1)
@@ -123,41 +127,169 @@
     narrow = jax.ShapeDtypeStruct(shape, jnp.bfloat16)
     outs = [wide] if mode == 3 else [narrow, wide]
     return pl.pallas_call(
-        functools.partial(step_kernel, mode, base, len(overflow) // 3),
+        functools.partial(step_kernel, mode, base, extras),
         out_shape=outs,
         grid_spec=pltpu.PrefetchScalarGridSpec(
             num_scalar_prefetch=2,
             grid=(capacity,),
             in_specs=[pl.BlockSpec(memory_space=pltpu.SMEM)]
-            + [pl.BlockSpec(memory_space=pl.ANY)] * (9 + len(overflow))
+            + [pl.BlockSpec(memory_space=pl.ANY)] * len(pieces)
             + [pl.BlockSpec((1, slots, rows, rows), lambda r, m, p: (live(r, m, p), 0, 0, 0))]
             + [panel_in] * len(panels),
             out_specs=[panel_out] * len(outs),
             scratch_shapes=[
                 pltpu.VMEM((9 * capacity, rows, cols), jnp.bfloat16),
                 pltpu.VMEM((rows, cols), jnp.float32),
-                pltpu.SemaphoreType.DMA((9 + len(overflow),)),
+                pltpu.SemaphoreType.DMA((9 + extras,)),
             ],
         ),
         compiler_params=pltpu.CompilerParams(vmem_limit_bytes=40 * 1024 * 1024),
         name=f"step{mode}",
-    )(meta, pattern, coeffs, *pieces, *overflow, blocks, *panels)
-
-
-def shifted(x, axis, by):
-    count = lax.axis_size(axis)
-    return lax.ppermute(x, axis, [(i, (i + by) % count) for i in range(count)])
-
-
-def halo_pieces(panels, base):
-    own = panels[:base]
-    above, below = shifted(own, "gx", 1), shifted(own, "gx", -1)
-    left, right = shifted(own, "gy", 1), shifted(own, "gy", -1)
-    return [
-        shifted(above, "gy", 1), above, shifted(above, "gy", -1),
-        left, panels, right,
-        shifted(below, "gy", 1), below, shifted(below, "gy", -1),
+    )(meta, pattern, coeffs, *pieces, blocks, *panels)
+
+
+def halo_kernel(base, tails, extras, heavy_ref, panels_ref, *refs):
+    halo_ref, refs = refs[0], refs[1:]
+    if extras:
+        extra_ref, near, own, middle, local_sem, extra_sems, keep_sem = refs[:7]
+        refs = refs[7:]
+    z_sems, row_sems, corner_sems = refs
+    row, col = lax.axis_index("gx"), lax.axis_index("gy")
+    rows, cols = lax.axis_size("gx"), lax.axis_size("gy")
+    vertical = ((lax.rem(row + 1, rows), col), (lax.rem(row + rows - 1, rows), col))
+    sideways = ((row, lax.rem(col + 1, cols)), (row, lax.rem(col + cols - 1, cols)))
+    barrier = pltpu.get_barrier_semaphore()
+    for target in vertical + sideways:
+        pl.semaphore_signal(barrier, inc=1, device_id=target, device_id_type=pl.DeviceIdType.MESH)
+    pl.semaphore_wait(barrier, 4)
+
+    def remote(src, dst, sems, target):
+        return pltpu.make_async_remote_copy(
+            src_ref=src,
+            dst_ref=dst,
+            send_sem=sems.at[0],
+            recv_sem=sems.at[1],
+            device_id=target,
+            device_id_type=pl.DeviceIdType.MESH,
+        )
+
+    half = (base + 1) // 2
+    chunks = [(0, half), (half, base - half)]
+    if extras:
+        for start, size in tails:
+            chunks.append((start, size))
+    z_copies, others = [], []
+    for n, (start, size) in enumerate(chunks):
+        pair = []
+        for v in range(2):
+            if start < base:
+                dst = halo_ref.at[6 * v + 1, pl.ds(start, size)]
+            else:
+                dst = near.at[v, pl.ds(start - base, size)]
+            pair.append(remote(panels_ref.at[pl.ds(start, size)], dst, z_sems.at[n, v], vertical[v]))
+        z_copies.append(pair)
+
+    def begin(copies):
+        for copy in copies:
+            copy.start()
+
+    begin(z_copies[0])
+    row_copies = [
+        remote(panels_ref.at[pl.ds(0, base)], halo_ref.at[3 + 2 * h], row_sems.at[h], sideways[h])
+        for h in range(2)
     ]
+    begin(row_copies)
+    others += row_copies
+    begin(z_copies[1])
+    if extras:
+        mine = pltpu.make_async_copy(panels_ref.at[pl.ds(base, own.shape[0])], own, local_sem)
+        mine.start()
+        mine.wait()
+    for n, (start, size) in enumerate(chunks):
+        for copy in z_copies[n]:
+            copy.wait_recv()
+        if n + 2 < len(chunks):
+            begin(z_copies[n + 2])
+        if start < base:
+            for v in range(2):
+                part = pl.ds(start, size)
+                copies = [
+                    remote(
+                        halo_ref.at[6 * v + 1, part],
+                        halo_ref.at[6 * v + 2 * h, part],
+                        corner_sems.at[n, v, h],
+                        sideways[h],
+                    )
+                    for h in range(2)
+                ]
+                begin(copies)
+                others += copies
+        else:
+            for e in range(extras):
+                away = heavy_ref[e]
+                for p in range(start - base, start - base + size):
+                    middle[e, p] = jnp.where(
+                        away == 0, near[0, p], jnp.where(away == 1, own[p], near[1, p])
+                    )
+                part = pl.ds(start - base, size)
+                copies = [
+                    remote(
+                        middle.at[e, part],
+                        extra_ref.at[e, 2 * h, part],
+                        extra_sems.at[n - 2, e, h],
+                        sideways[h],
+                    )
+                    for h in range(2)
+                ]
+                begin(copies)
+                others += copies
+    if extras:
+        kept = [
+            pltpu.make_async_copy(middle.at[e], extra_ref.at[e, 1], keep_sem.at[e]) for e in range(extras)
+        ]
+        begin(kept)
+        for copy in kept:
+            copy.wait()
+    for pair in z_copies:
+        for copy in pair:
+            copy.wait_send()
+    for copy in others:
+        copy.wait()
+
+
+def halo(panels, base, heavy_rows):
+    capacity, rows, cols = panels.shape
+    extras, rest = len(heavy_rows), capacity - base
+    dma = pltpu.SemaphoreType.DMA
+    outs = [jax.ShapeDtypeStruct((9, base, rows, cols), panels.dtype)]
+    scratch, tails = [], []
+    if extras:
+        half = (rest + 1) // 2
+        tails = [(base, half), (base + half, rest - half)]
+        outs.append(jax.ShapeDtypeStruct((extras, 3, rest, rows, cols), panels.dtype))
+        scratch = [
+            pltpu.VMEM((2, rest, rows, cols), panels.dtype),
+            pltpu.VMEM((rest, rows, cols), panels.dtype),
+            pltpu.VMEM((extras, rest, rows, cols), panels.dtype),
+            dma,
+            dma((2, extras, 2, 2)),
+            dma((extras,)),
+        ]
+    scratch += [dma((4, 2, 2)), dma((2, 2)), dma((2, 2, 2, 2))]
+    away = jnp.stack(heavy_rows) if extras else jnp.zeros((1,), jnp.int32)
+    return pl.pallas_call(
+        functools.partial(halo_kernel, base, tails, extras),
+        out_shape=outs,
+        in_specs=[pl.BlockSpec(memory_space=pltpu.SMEM), pl.BlockSpec(memory_space=pl.ANY)],
+        out_specs=[pl.BlockSpec(memory_space=pl.ANY)] * len(outs),
+        scratch_shapes=scratch,
+        compiler_params=pltpu.CompilerParams(
+            collective_id=0 if extras else 1,
+            has_side_effects=True,
+            vmem_limit_bytes=32 * 1024 * 1024,
+        ),
+        name="halo_part" if extras else "halo_full",
+    )(away.astype(jnp.int32), panels)
 
 
 def local(counts, probes, blocks, pattern, coeffs):
@@ -184,25 +316,18 @@
     rows, table = blocks[0, 0], pattern[0, 0]
 
     def expand(base, heavy, start):
-        meta = [my_count]
+        meta, heavy_rows = [my_count], []
         for d in heavy:
             di = (d // grid_cols - my_row + 1) % grid_rows
             dj = (d % grid_cols - my_col + 1) % grid_cols
             near = (d >= 0) & (di < 3) & (dj < 3) & (d != my_domain)
+            heavy_rows.append(di)
             meta.append(jnp.where(near, di * 3 + dj, -1))
         meta = jnp.stack(meta).astype(jnp.int32)
 
         def run(mode, panels, *rest):
-            pieces = halo_pieces(panels, base)
-            overflow = []
-            if heavy:
-                own = panels[base:]
-                above, below = shifted(own, "gx", 1), shifted(own, "gx", -1)
-            for d in heavy:
-                row = (d // grid_cols - my_row + 1) % grid_rows
-                middle = jnp.where(row == 0, above, jnp.where(row == 1, own, below))
-                overflow += [shifted(middle, "gy", 1), middle, shifted(middle, "gy", -1)]
-            return step(mode, base, meta, table, coeffs, pieces, overflow, rows, rest)
+            ring, *extra = halo(panels, base, heavy_rows)
+            return step(mode, base, meta, table, coeffs, [panels, ring] + extra, rows, rest)
 
         sent, one = run(1, start)
         sent, two = run(2, sent, start)

time: 426 us -> 350 us (0.82)
  the two profiles are of different devices: /device:TPU:0 before, /device:TPU:1 now
where the time goes in v3:
time: 350 us; the launch traced here: 347 us
  Pallas kernels  276 us (79%)
  waiting for transfers between devices  34.8 us (10%)
  local copies, waits for them, and re-layouts  19.5 us (6%)
  starting transfers between devices  7.1 us (2%)
  loops' own time  4.05 us (1%)
  other arithmetic  3.6 us (1%)
    pallas_call x3, Pallas kernels, halo(): pl.pallas_call(functools.partial(halo_kernel, base, tails, extras), out_s...  243 us
    all_to_all x1, waiting for transfers between devices, local(): lax.all_to_all(outgoing, ('gx', 'gy'), split_axis=0, concat_axis=3, tiled...  34.8 us
    pallas_call x3, Pallas kernels, step(): pl.pallas_call(functools.partial(step_kernel, mode, base, extras), out_sh...  31.1 us
    cond x12, local copies, waits for them, and re-layouts  9.54 us
    all_to_all x1, starting transfers between devices, local(): lax.all_to_all(outgoing, ('gx', 'gy'), split_axis=0, concat_axis=3, tiled...  7.1 us
  transfers between devices with their start and end apart: 1, of which 1 were waited for; matrix products, arithmetic and copies ran while one was open for 0% of the time, Pallas kernels for 0%

profile of v3, /device:TPU:1, one launch (start us, length us, event | category | flops | bytes accessed | tf_op | source)
XLA Modules:
  0.0 347.4 jit_solution(2312745701671751029)
XLA Ops:
  0.0 0.8 select_reduce_fusion
  0.8 3.1 copy.14
  3.9 0.7 fusion.6
  4.7 1.4 pack.1
  6.1 1.7 copy-done.3
  7.7 4.4 %copy.15 = bf16[32,3,128,64]{2,3,1,0:T(8,128)(2,1)} copy(bf16[32,3,128,64]{3,2,1,0:T(8,128)(2,1)} %copy-done.3) | data formatting | bytes 3145728 | tf_op jit(solution)/shard_map/pack/pallas_call | solution.py:27
  12.1 7.1 %all-to-all-start = ((bf16[32,3,128,64]{2,3,1,0:T(8,128)(2,1)}), bf16[32,3,128,64]{2,3,1,0:T(8,128)(2,1)S(1)}, u32[]{:S(2)}, u32[]{:S(2)}) async-start(bf16[32,3,128,64]{2,3,1,0:T(8,128)(2,1)} %copy.15), calls=%async_computation | async-start | bytes 3145728 | tf_op jit(solution)/shard_map/all_to_all | solution.py:311
  21.6 34.8 %all-to-all-done = bf16[32,3,128,64]{2,3,1,0:T(8,128)(2,1)S(1)} async-done(((bf16[32,3,128,64]{2,3,1,0:T(8,128)(2,1)}), bf16[32,3,128,64]{2,3,1,0:T(8,128)(2,1)S(1)}, u32[]{:S(2)}, u32[]{:S(2)}) %all-to-all-start) | async-done | bytes 1572896 | tf_op jit(solution)/shard_map/all_to_all | solution.py:311
  56.3 0.1 copy.16
  56.5 0.6 fusion.1
  57.0 0.7 copy.17
  57.8 289.6 %conditional.1 = (f32[1,1,12,128,512]{4,3,2,1,0:T(8,128)}) conditional(s32[]{:T(128)} %convert_element_type.10, (s32[]{:T(128)}, bf16[12,128,512]{2,1,0:T(8,128)(2,1)S(1)}, s32[12,24]{1,0:T(8,128)S(1)}, f32[4]{0:T(128)S(1)}, bf16[12,24,128,128]{3,2,1,0:T(8,128)(2,1)}) %tuple.34, (s32[]{:T(128)}, s32[32,32]{1,0:T(8,128)S(1)}, s32[32]{0:T(128)S(1)}, ...), branch_computations={%region_4.5_spmd, %region_5.8_spmd} | conditional | flops 1176 | bytes 220201152 | solution.py:342
  57.8 0.1 reduce_sum.42
  57.9 0.6 fusion
  62.5 0.7 pad_add_fusion.meta_ref
  63.2 79.9 %halo_part.6 = (bf16[9,7,128,512]{3,2,1,0:T(8,128)(2,1)S(1)}, bf16[1,3,5,128,512]{4,3,2,1,0:T(8,128)(2,1)S(1)}) custom-call(s32[1]{0:T(128)} %bitcast.4.heavy_ref, bf16[12,128,512]{2,1,0:T(8,128)(2,1)S(1)} %get-tuple-element.96.panels_ref.refs_0_.refs_4_), custom_call_target="tpu_custom_call" | custom-call | tf_op jit(solution)/shard_map/cond/branch_1_fun/halo_part/pallas_call | solution.py:280
  143.1 3.2 copy-done.4
  146.3 11.3 %step1.4 = (bf16[12,128,512]{2,1,0:T(8,128)(2,1)S(1)}, f32[12,128,512]{2,1,0:T(8,128)S(1)}) custom-call(s32[2]{0:T(128)S(1)} %pad_add_fusion.meta_ref, s32[12,24]{1,0:T(8,128)S(1)} %get-tuple-element.94.pattern_ref, f32[4]{0:T(128)S(1)} %get-tuple-element.95.coeffs_ref, bf16[12,128,512]{2,1,0:T(8,128)(2,1)S(1)} %get-tuple-element.96.panels_ref.refs_0_.refs_4_, ...), custom_call_target="tpu_custom_call" | custom-call | tf_op jit(solution)/shard_map/cond/branch_1_fun/step1/pallas_call | solution.py:129
  157.7 81.1 %halo_part.7 = (bf16[9,7,128,512]{3,2,1,0:T(8,128)(2,1)S(1)}, bf16[1,3,5,128,512]{4,3,2,1,0:T(8,128)(2,1)S(1)}) custom-call(s32[1]{0:T(128)} %bitcast.4.heavy_ref, bf16[12,128,512]{2,1,0:T(8,128)(2,1)S(1)} %get-tuple-element.100.panels_ref.refs_0_), custom_call_target="tpu_custom_call" | custom-call | tf_op jit(solution)/shard_map/cond/branch_1_fun/halo_part/pallas_call | solution.py:280
  238.7 3.2 copy-done.6
  241.9 8.5 %step2.4 = (bf16[12,128,512]{2,1,0:T(8,128)(2,1)S(1)}, f32[12,128,512]{2,1,0:T(8,128)S(1)}) custom-call(s32[2]{0:T(128)S(1)} %pad_add_fusion.meta_ref, s32[12,24]{1,0:T(8,128)S(1)} %get-tuple-element.94.pattern_ref, f32[4]{0:T(128)S(1)} %get-tuple-element.95.coeffs_ref, bf16[12,128,512]{2,1,0:T(8,128)(2,1)S(1)} %get-tuple-element.100.panels_ref.refs_0_, ...), custom_call_target="tpu_custom_call" | custom-call | tf_op jit(solution)/shard_map/cond/branch_1_fun/step2/pallas_call | solution.py:129
  250.4 82.5 %halo_part.8 = (bf16[9,7,128,512]{3,2,1,0:T(8,128)(2,1)S(1)}, bf16[1,3,5,128,512]{4,3,2,1,0:T(8,128)(2,1)S(1)}) custom-call(s32[1]{0:T(128)} %bitcast.4.heavy_ref, bf16[12,128,512]{2,1,0:T(8,128)(2,1)S(1)} %get-tuple-element.103.panels_ref.refs_0_), custom_call_target="tpu_custom_call" | custom-call | tf_op jit(solution)/shard_map/cond/branch_1_fun/halo_part/pallas_call | solution.py:280
  333.0 3.2 copy-done.5
  336.1 11.2 %step3.4 = f32[12,128,512]{2,1,0:T(8,128)} custom-call(s32[2]{0:T(128)S(1)} %pad_add_fusion.meta_ref, s32[12,24]{1,0:T(8,128)S(1)} %get-tuple-element.94.pattern_ref, f32[4]{0:T(128)S(1)} %get-tuple-element.95.coeffs_ref, bf16[12,128,512]{2,1,0:T(8,128)(2,1)S(1)} %get-tuple-element.103.panels_ref.refs_0_, bf16[9,7,128,512]{3,2,1,0:T(8,128)(2,1)} %copy-done.5, ...), custom_call_target="tpu_custom_call" | custom-call | tf_op jit(solution)/shard_map/cond/branch_1_fun/step3/pallas_call | solution.py:129
  (23 shorter events, 0.1 us)
Async XLA Ops:
  0.0 3.9 %copy-start.12 = (s32[32]{0:T(128)S(1)}, s32[32]{0:T(128)}, u32[]{:S(2)}) copy-start(s32[32]{0:T(128)} %param.7) | copy-start | bytes 388
  6.1 1.7 copy-start.3
  7.7 13.8 %copy-start.11 = (s32[1,1,12,24]{3,1,2,0:T(1,128)S(1)}, s32[1,1,12,24]{3,1,2,0:T(1,128)}, u32[]{:S(2)}) copy-start(s32[1,1,12,24]{3,1,2,0:T(1,128)} %param.10) | copy-start | bytes 3460
  12.1 44.2 %all-to-all-start = ((bf16[32,3,128,64]{2,3,1,0:T(8,128)(2,1)}), bf16[32,3,128,64]{2,3,1,0:T(8,128)(2,1)S(1)}, u32[]{:S(2)}, u32[]{:S(2)}) async-start(bf16[32,3,128,64]{2,3,1,0:T(8,128)(2,1)} %copy.15), calls=%async_computation | async-start | bytes 3145728 | tf_op jit(solution)/shard_map/all_to_all | solution.py:311
  56.5 1.3 copy-start.10
  143.1 3.2 copy-start.4
  146.3 95.6 %slice-start = ((s8[9437184]{0:T(1024)(128)(4,1)}), s8[4194304]{0:T(1024)(128)(4,1)S(1)}, s32[]{:S(2)}) async-start(s8[9437184]{0:T(1024)(128)(4,1)} %bitcast.22), calls=%async_computation.1 | async-start | bytes 8388608 | tf_op jit(solution)/shard_map/cond
  146.3 95.6 %slice-start.1 = ((s8[9437184]{0:T(1024)(128)(4,1)}), s8[4194304]{0:T(1024)(128)(4,1)S(1)}, s32[]{:S(2)}) async-start(s8[9437184]{0:T(1024)(128)(4,1)} %bitcast.22), calls=%async_computation.2 | async-start | bytes 8388608 | tf_op jit(solution)/shard_map/cond
  146.3 95.6 %slice-start.2 = ((s8[9437184]{0:T(1024)(128)(4,1)}), s8[1048576]{0:T(1024)(128)(4,1)S(1)}, s32[]{:S(2)}) async-start(s8[9437184]{0:T(1024)(128)(4,1)} %bitcast.22), calls=%async_computation.3 | async-start | bytes 2097152 | tf_op jit(solution)/shard_map/cond
  238.7 3.2 copy-start.6
  333.0 3.2 copy-start.5

commit v4 on v3

--- a/solution.py
+++ b/solution.py
@@ -143,12 +143,21 @@
                 pltpu.SemaphoreType.DMA((9 + extras,)),
             ],
         ),
-        compiler_params=pltpu.CompilerParams(vmem_limit_bytes=40 * 1024 * 1024),
+        compiler_params=pltpu.CompilerParams(vmem_limit_bytes=58 * 1024 * 1024),
         name=f"step{mode}",
     )(meta, pattern, coeffs, *pieces, blocks, *panels)
 
 
-def halo_kernel(base, tails, extras, heavy_ref, panels_ref, *refs):
+PARTS = 3
+AHEAD = 3
+
+
+def cut(low, high):
+    edges = [low + -((low - high) * n // PARTS) for n in range(PARTS + 1)]
+    return [(a, b - a) for a, b in zip(edges, edges[1:]) if b > a]
+
+
+def halo_kernel(base, extras, heavy_ref, panels_ref, *refs):
     halo_ref, refs = refs[0], refs[1:]
     if extras:
         extra_ref, near, own, middle, local_sem, extra_sems, keep_sem = refs[:7]
@@ -173,11 +182,10 @@
             device_id_type=pl.DeviceIdType.MESH,
         )
 
-    half = (base + 1) // 2
-    chunks = [(0, half), (half, base - half)]
-    if extras:
-        for start, size in tails:
-            chunks.append((start, size))
+    chunks = cut(0, base)
+    first_tail = len(chunks)
+    if extras:
+        chunks += cut(base, panels_ref.shape[0])
     z_copies, others = [], []
     for n, (start, size) in enumerate(chunks):
         pair = []
@@ -200,7 +208,8 @@
     ]
     begin(row_copies)
     others += row_copies
-    begin(z_copies[1])
+    for pair in z_copies[1:AHEAD]:
+        begin(pair)
     if extras:
         mine = pltpu.make_async_copy(panels_ref.at[pl.ds(base, own.shape[0])], own, local_sem)
         mine.start()
@@ -208,8 +217,8 @@
     for n, (start, size) in enumerate(chunks):
         for copy in z_copies[n]:
             copy.wait_recv()
-        if n + 2 < len(chunks):
-            begin(z_copies[n + 2])
+        if n + AHEAD < len(chunks):
+            begin(z_copies[n + AHEAD])
         if start < base:
             for v in range(2):
                 part = pl.ds(start, size)
@@ -236,7 +245,7 @@
                     remote(
                         middle.at[e, part],
                         extra_ref.at[e, 2 * h, part],
-                        extra_sems.at[n - 2, e, h],
+                        extra_sems.at[n - first_tail, e, h],
                         sideways[h],
                     )
                     for h in range(2)
@@ -262,23 +271,21 @@
     extras, rest = len(heavy_rows), capacity - base
     dma = pltpu.SemaphoreType.DMA
     outs = [jax.ShapeDtypeStruct((9, base, rows, cols), panels.dtype)]
-    scratch, tails = [], []
-    if extras:
-        half = (rest + 1) // 2
-        tails = [(base, half), (base + half, rest - half)]
+    scratch = []
+    if extras:
         outs.append(jax.ShapeDtypeStruct((extras, 3, rest, rows, cols), panels.dtype))
         scratch = [
             pltpu.VMEM((2, rest, rows, cols), panels.dtype),
             pltpu.VMEM((rest, rows, cols), panels.dtype),
             pltpu.VMEM((extras, rest, rows, cols), panels.dtype),
             dma,
-            dma((2, extras, 2, 2)),
+            dma((PARTS, extras, 2, 2)),
             dma((extras,)),
         ]
-    scratch += [dma((4, 2, 2)), dma((2, 2)), dma((2, 2, 2, 2))]
+    scratch += [dma((2 * PARTS, 2, 2)), dma((2, 2)), dma((PARTS, 2, 2, 2))]
     away = jnp.stack(heavy_rows) if extras else jnp.zeros((1,), jnp.int32)
     return pl.pallas_call(
-        functools.partial(halo_kernel, base, tails, extras),
+        functools.partial(halo_kernel, base, extras),
         out_shape=outs,
         in_specs=[pl.BlockSpec(memory_space=pltpu.SMEM), pl.BlockSpec(memory_space=pl.ANY)],
         out_specs=[pl.BlockSpec(memory_space=pl.ANY)] * len(outs),
@@ -286,7 +293,7 @@
         compiler_params=pltpu.CompilerParams(
             collective_id=0 if extras else 1,
             has_side_effects=True,
-            vmem_limit_bytes=32 * 1024 * 1024,
+            vmem_limit_bytes=58 * 1024 * 1024,
         ),
         name="halo_part" if extras else "halo_full",
     )(away.astype(jnp.int32), panels)

time: 350 us -> 342 us (0.977)
  local copies, waits for them, and re-layouts: 19.5 us -> 9.94 us
    cond x12 -> x0, local copies, waits for them, and re-layouts: 9.54 us -> none
    pallas_call x3, Pallas kernels: 243 us -> 235 us  [halo(): pl.pallas_call(functools.partial(halo_kernel, base, extras), out_shape=ou...]
    pallas_call x3, Pallas kernels: 31.1 us -> 37.4 us  [step(): pl.pallas_call(functools.partial(step_kernel, mode, base, extras), out_sh...]
where the time goes in v4:
time: 342 us; the launch traced here: 336 us
  Pallas kernels  274 us (80%)
  waiting for transfers between devices  34.6 us (10%)
  local copies, waits for them, and re-layouts  9.94 us (3%)
  starting transfers between devices  7.1 us (2%)
  other arithmetic  4.24 us (1%)
  loops' own time  4.02 us (1%)
    pallas_call x3, Pallas kernels, halo(): pl.pallas_call(functools.partial(halo_kernel, base, extras), out_shape=ou...  235 us
    pallas_call x3, Pallas kernels, step(): pl.pallas_call(functools.partial(step_kernel, mode, base, extras), out_sh...  37.4 us
    all_to_all x1, waiting for transfers between devices, local(): lax.all_to_all(outgoing, ('gx', 'gy'), split_axis=0, concat_axis=3, tiled...  34.6 us
    all_to_all x1, starting transfers between devices, local(): lax.all_to_all(outgoing, ('gx', 'gy'), split_axis=0, concat_axis=3, tiled...  7.1 us
  transfers between devices with their start and end apart: 1, of which 1 were waited for; matrix products, arithmetic and copies ran while one was open for 0% of the time, Pallas kernels for 0%

profile of v4, /device:TPU:1, one launch (start us, length us, event | category | flops | bytes accessed | tf_op | source)
XLA Modules:
  0.0 336.4 jit_solution(5952722848834488746)
XLA Ops:
  0.0 0.8 select_reduce_fusion
  0.8 3.1 copy.14
  3.9 0.0 copy-done.3
  3.9 0.7 fusion.6
  4.7 1.4 pack.1
  6.1 0.0 copy-start
  6.1 1.7 copy-done
  7.8 4.4 %copy.15 = bf16[32,3,128,64]{2,3,1,0:T(8,128)(2,1)} copy(bf16[32,3,128,64]{3,2,1,0:T(8,128)(2,1)} %copy-done) | data formatting | bytes 3145728 | tf_op jit(solution)/shard_map/pack/pallas_call | solution.py:27
  12.1 7.1 %all-to-all-start = ((bf16[32,3,128,64]{2,3,1,0:T(8,128)(2,1)}), bf16[32,3,128,64]{2,3,1,0:T(8,128)(2,1)S(1)}, u32[]{:S(2)}, u32[]{:S(2)}) async-start(bf16[32,3,128,64]{2,3,1,0:T(8,128)(2,1)} %copy.15), calls=%async_computation | async-start | bytes 3145728 | tf_op jit(solution)/shard_map/all_to_all | solution.py:318
  21.8 34.6 %all-to-all-done = bf16[32,3,128,64]{2,3,1,0:T(8,128)(2,1)S(1)} async-done(((bf16[32,3,128,64]{2,3,1,0:T(8,128)(2,1)}), bf16[32,3,128,64]{2,3,1,0:T(8,128)(2,1)S(1)}, u32[]{:S(2)}, u32[]{:S(2)}) %all-to-all-start) | async-done | bytes 1572896 | tf_op jit(solution)/shard_map/all_to_all | solution.py:318
  56.4 0.1 copy.16
  56.5 0.0 copy-start.1
  56.5 0.6 fusion.1
  57.1 0.7 copy.17
  57.8 278.5 %conditional.1 = (f32[1,1,12,128,512]{4,3,2,1,0:T(8,128)}) conditional(s32[]{:T(128)} %convert_element_type.10, (s32[]{:T(128)}, bf16[12,128,512]{2,1,0:T(8,128)(2,1)S(1)}, s32[12,24]{1,0:T(8,128)S(1)}, f32[4]{0:T(128)S(1)}, bf16[12,24,128,128]{3,2,1,0:T(8,128)(2,1)}) %tuple.34, (s32[]{:T(128)}, s32[32,32]{1,0:T(8,128)S(1)}, s32[32]{0:T(128)S(1)}, ...), branch_computations={%region_4.5_spmd, %region_5.8_spmd} | conditional | flops 1176 | bytes 5335 | solution.py:349
  57.9 0.1 reduce_sum.42
  58.0 0.6 fusion
  62.6 1.3 pad_add_fusion.meta_ref
  63.9 77.7 %halo_part.6 = (bf16[9,7,128,512]{3,2,1,0:T(8,128)(2,1)}, bf16[1,3,5,128,512]{4,3,2,1,0:T(8,128)(2,1)}) custom-call(s32[1]{0:T(128)} %bitcast.4.heavy_ref, bf16[12,128,512]{2,1,0:T(8,128)(2,1)S(1)} %get-tuple-element.96.panels_ref.refs_0_.refs_4_), custom_call_target="tpu_custom_call" | custom-call | tf_op jit(solution)/shard_map/cond/branch_1_fun/halo_part/pallas_call | solution.py:287
  141.6 12.1 %step1.4 = (bf16[12,128,512]{2,1,0:T(8,128)(2,1)}, f32[12,128,512]{2,1,0:T(8,128)}) custom-call(s32[2]{0:T(128)} %pad_add_fusion.meta_ref, s32[12,24]{1,0:T(8,128)S(1)} %get-tuple-element.94.pattern_ref, f32[4]{0:T(128)S(1)} %get-tuple-element.95.coeffs_ref, bf16[12,128,512]{2,1,0:T(8,128)(2,1)S(1)} %get-tuple-element.96.panels_ref.refs_0_.refs_4_, ...), custom_call_target="tpu_custom_call" | custom-call | tf_op jit(solution)/shard_map/cond/branch_1_fun/step1/pallas_call | solution.py:129
  153.7 80.1 %halo_part.7 = (bf16[9,7,128,512]{3,2,1,0:T(8,128)(2,1)}, bf16[1,3,5,128,512]{4,3,2,1,0:T(8,128)(2,1)}) custom-call(s32[1]{0:T(128)} %bitcast.4.heavy_ref, bf16[12,128,512]{2,1,0:T(8,128)(2,1)} %get-tuple-element.100.panels_ref.refs_0_), custom_call_target="tpu_custom_call" | custom-call | tf_op jit(solution)/shard_map/cond/branch_1_fun/halo_part/pallas_call | solution.py:287
  233.8 12.6 %step2.4 = (bf16[12,128,512]{2,1,0:T(8,128)(2,1)}, f32[12,128,512]{2,1,0:T(8,128)}) custom-call(s32[2]{0:T(128)} %pad_add_fusion.meta_ref, s32[12,24]{1,0:T(8,128)S(1)} %get-tuple-element.94.pattern_ref, f32[4]{0:T(128)S(1)} %get-tuple-element.95.coeffs_ref, bf16[12,128,512]{2,1,0:T(8,128)(2,1)} %get-tuple-element.100.panels_ref.refs_0_, ...), custom_call_target="tpu_custom_call" | custom-call | tf_op jit(solution)/shard_map/cond/branch_1_fun/step2/pallas_call | solution.py:129
  246.5 77.2 %halo_part.8 = (bf16[9,7,128,512]{3,2,1,0:T(8,128)(2,1)}, bf16[1,3,5,128,512]{4,3,2,1,0:T(8,128)(2,1)}) custom-call(s32[1]{0:T(128)} %bitcast.4.heavy_ref, bf16[12,128,512]{2,1,0:T(8,128)(2,1)} %get-tuple-element.103.panels_ref.refs_0_), custom_call_target="tpu_custom_call" | custom-call | tf_op jit(solution)/shard_map/cond/branch_1_fun/halo_part/pallas_call | solution.py:287
  323.7 12.7 %step3.4 = f32[12,128,512]{2,1,0:T(8,128)} custom-call(s32[2]{0:T(128)} %pad_add_fusion.meta_ref, s32[12,24]{1,0:T(8,128)S(1)} %get-tuple-element.94.pattern_ref, f32[4]{0:T(128)S(1)} %get-tuple-element.95.coeffs_ref, bf16[12,128,512]{2,1,0:T(8,128)(2,1)} %get-tuple-element.103.panels_ref.refs_0_, bf16[9,7,128,512]{3,2,1,0:T(8,128)(2,1)} %get-tuple-element.104.refs_1_, ...), custom_call_target="tpu_custom_call" | custom-call | tf_op jit(solution)/shard_map/cond/branch_1_fun/step3/pallas_call | solution.py:129
  (10 shorter events, 0.0 us)
Async XLA Ops:
  0.0 3.9 %copy-start.3 = (s32[32]{0:T(128)S(1)}, s32[32]{0:T(128)}, u32[]{:S(2)}) copy-start(s32[32]{0:T(128)} %param.7) | copy-start | bytes 388
  6.1 1.7 copy-start
  7.8 13.9 %copy-start.2 = (s32[1,1,12,24]{3,1,2,0:T(1,128)S(1)}, s32[1,1,12,24]{3,1,2,0:T(1,128)}, u32[]{:S(2)}) copy-start(s32[1,1,12,24]{3,1,2,0:T(1,128)} %param.10) | copy-start | bytes 3460
  12.1 44.2 %all-to-all-start = ((bf16[32,3,128,64]{2,3,1,0:T(8,128)(2,1)}), bf16[32,3,128,64]{2,3,1,0:T(8,128)(2,1)S(1)}, u32[]{:S(2)}, u32[]{:S(2)}) async-start(bf16[32,3,128,64]{2,3,1,0:T(8,128)(2,1)} %copy.15), calls=%async_computation | async-start | bytes 3145728 | tf_op jit(solution)/shard_map/all_to_all | solution.py:318
  56.5 1.3 copy-start.1

commit v5 on v4

--- a/solution.py
+++ b/solution.py
@@ -157,7 +157,7 @@
     return [(a, b - a) for a, b in zip(edges, edges[1:]) if b > a]
 
 
-def halo_kernel(base, extras, heavy_ref, panels_ref, *refs):
+def halo_kernel(base, extras, parity, heavy_ref, panels_ref, *refs):
     halo_ref, refs = refs[0], refs[1:]
     if extras:
         extra_ref, near, own, middle, local_sem, extra_sems, keep_sem = refs[:7]
@@ -186,7 +186,7 @@
     first_tail = len(chunks)
     if extras:
         chunks += cut(base, panels_ref.shape[0])
-    z_copies, others = [], []
+    z_copies, others, tail_copies = [], [], []
     for n, (start, size) in enumerate(chunks):
         pair = []
         for v in range(2):
@@ -197,9 +197,31 @@
             pair.append(remote(panels_ref.at[pl.ds(start, size)], dst, z_sems.at[n, v], vertical[v]))
         z_copies.append(pair)
 
+    holds = None if parity is None else lax.rem(col, 2) == parity
+
+    def holder(act, other=False):
+        if holds is None:
+            act()
+        else:
+            pl.when(jnp.logical_not(holds) if other else holds)(act)
+
+    def tail_only(n, act):
+        if chunks[n][0] < base:
+            act()
+        else:
+            holder(act)
+
     def begin(copies):
         for copy in copies:
             copy.start()
+
+    def arrive(copies):
+        for copy in copies:
+            copy.wait_recv()
+
+    def leave(copies):
+        for copy in copies:
+            copy.wait_send()
 
     begin(z_copies[0])
     row_copies = [
@@ -208,17 +230,16 @@
     ]
     begin(row_copies)
     others += row_copies
-    for pair in z_copies[1:AHEAD]:
-        begin(pair)
+    for n in range(1, min(AHEAD, len(chunks))):
+        tail_only(n, lambda n=n: begin(z_copies[n]))
     if extras:
         mine = pltpu.make_async_copy(panels_ref.at[pl.ds(base, own.shape[0])], own, local_sem)
         mine.start()
         mine.wait()
     for n, (start, size) in enumerate(chunks):
-        for copy in z_copies[n]:
-            copy.wait_recv()
+        tail_only(n, lambda: arrive(z_copies[n]))
         if n + AHEAD < len(chunks):
-            begin(z_copies[n + AHEAD])
+            tail_only(n + AHEAD, lambda: begin(z_copies[n + AHEAD]))
         if start < base:
             for v in range(2):
                 part = pl.ds(start, size)
@@ -234,39 +255,49 @@
                 begin(copies)
                 others += copies
         else:
-            for e in range(extras):
-                away = heavy_ref[e]
-                for p in range(start - base, start - base + size):
-                    middle[e, p] = jnp.where(
-                        away == 0, near[0, p], jnp.where(away == 1, own[p], near[1, p])
-                    )
-                part = pl.ds(start - base, size)
-                copies = [
-                    remote(
-                        middle.at[e, part],
-                        extra_ref.at[e, 2 * h, part],
-                        extra_sems.at[n - first_tail, e, h],
-                        sideways[h],
-                    )
-                    for h in range(2)
-                ]
+            copies = [
+                remote(
+                    middle.at[e, pl.ds(start - base, size)],
+                    extra_ref.at[e, 2 * h, pl.ds(start - base, size)],
+                    extra_sems.at[n - first_tail, e, h],
+                    sideways[h],
+                )
+                for e in range(extras)
+                for h in range(2)
+            ]
+
+            def forward(start=start, size=size, copies=copies):
+                for e in range(extras):
+                    away = heavy_ref[e]
+                    for p in range(start - base, start - base + size):
+                        middle[e, p] = jnp.where(
+                            away == 0, near[0, p], jnp.where(away == 1, own[p], near[1, p])
+                        )
                 begin(copies)
-                others += copies
+
+            holder(forward)
+            tail_copies += copies
     if extras:
         kept = [
             pltpu.make_async_copy(middle.at[e], extra_ref.at[e, 1], keep_sem.at[e]) for e in range(extras)
         ]
-        begin(kept)
-        for copy in kept:
-            copy.wait()
-    for pair in z_copies:
-        for copy in pair:
-            copy.wait_send()
+
+        def keep():
+            begin(kept)
+            for copy in kept:
+                copy.wait()
+
+        holder(keep)
+    for n in range(len(chunks)):
+        tail_only(n, lambda: leave(z_copies[n]))
     for copy in others:
         copy.wait()
-
-
-def halo(panels, base, heavy_rows):
+    if extras:
+        holder(lambda: leave(tail_copies))
+        holder(lambda: arrive(tail_copies), other=True)
+
+
+def halo(panels, base, heavy_rows, parity):
     capacity, rows, cols = panels.shape
     extras, rest = len(heavy_rows), capacity - base
     dma = pltpu.SemaphoreType.DMA
@@ -285,13 +316,13 @@
     scratch += [dma((2 * PARTS, 2, 2)), dma((2, 2)), dma((PARTS, 2, 2, 2))]
     away = jnp.stack(heavy_rows) if extras else jnp.zeros((1,), jnp.int32)
     return pl.pallas_call(
-        functools.partial(halo_kernel, base, extras),
+        functools.partial(halo_kernel, base, extras, parity),
         out_shape=outs,
         in_specs=[pl.BlockSpec(memory_space=pltpu.SMEM), pl.BlockSpec(memory_space=pl.ANY)],
         out_specs=[pl.BlockSpec(memory_space=pl.ANY)] * len(outs),
         scratch_shapes=scratch,
         compiler_params=pltpu.CompilerParams(
-            collective_id=0 if extras else 1,
+            collective_id=3 if not extras else 2 if parity is None else parity,
             has_side_effects=True,
             vmem_limit_bytes=58 * 1024 * 1024,
         ),
@@ -322,7 +353,7 @@
     start = start.reshape(per_peer * grid_rows, panel_rows, probe_cols)[:capacity]
     rows, table = blocks[0, 0], pattern[0, 0]
 
-    def expand(base, heavy, start):
+    def expand(base, heavy, parity, start):
         meta, heavy_rows = [my_count], []
         for d in heavy:
             di = (d // grid_cols - my_row + 1) % grid_rows
@@ -333,7 +364,7 @@
         meta = jnp.stack(meta).astype(jnp.int32)
 
         def run(mode, panels, *rest):
-            ring, *extra = halo(panels, base, heavy_rows)
+            ring, *extra = halo(panels, base, heavy_rows, parity)
             return step(mode, base, meta, table, coeffs, [panels, ring] + extra, rows, rest)
 
         sent, one = run(1, start)
@@ -346,12 +377,19 @@
     over = counts > base
     rank = jnp.sum(jnp.where(ids[None, :] < ids[:, None], over[None, :], False), axis=1)
     heavy = [jnp.max(jnp.where(over & (rank == h), ids, -1)) for h in range(extras)]
-    out = lax.cond(
-        jnp.sum(over) <= extras,
-        lambda s: expand(base, heavy, s),
-        lambda s: expand(capacity, [], s),
-        start,
-    )
+    odd = sum(jnp.where((d >= 0) & (d % grid_cols % 2 == 1), 1, 0) for d in heavy)
+    even = sum(jnp.where((d >= 0) & (d % grid_cols % 2 == 0), 1, 0) for d in heavy)
+    branches = [
+        lambda s: expand(capacity, [], None, s),
+        lambda s: expand(base, heavy, None, s),
+    ]
+    which = jnp.where(jnp.sum(over) <= extras, 1, 0)
+    if grid_cols % 2 == 0:
+        branches += [lambda s: expand(base, heavy, 0, s), lambda s: expand(base, heavy, 1, s)]
+        which = jnp.where(which == 0, 0, jnp.where(odd == 0, 2, jnp.where(even == 0, 3, 1)))
+    if extras == 1 and grid_cols % 2 == 0:
+        branches[1] = branches[0]
+    out = lax.switch(which, branches, start)
     return out[None, None]
 
 

time: 342 us -> 320 us (0.936); the launches traced: 336 us -> 320 us
  Pallas kernels: 274 us -> 257 us
    pallas_call x3, Pallas kernels: 235 us -> 204 us  [halo(): pl.pallas_call(functools.partial(halo_kernel, base, extras, parity), out_...]
    pallas_call x3, Pallas kernels: 37.4 us -> 52.1 us  [step(): pl.pallas_call(functools.partial(step_kernel, mode, base, extras), out_sh...]
where the time goes in v5:
time: 320 us
  Pallas kernels  257 us (80%)
  waiting for transfers between devices  31.8 us (10%)
  local copies, waits for them, and re-layouts  9.92 us (3%)
  starting transfers between devices  7.1 us (2%)
  between operations  5.43 us (2%)
  other arithmetic  4.18 us (1%)
  loops' own time  3.97 us (1%)
    pallas_call x3, Pallas kernels, halo(): pl.pallas_call(functools.partial(halo_kernel, base, extras, parity), out_...  204 us
    pallas_call x3, Pallas kernels, step(): pl.pallas_call(functools.partial(step_kernel, mode, base, extras), out_sh...  52.1 us
    all_to_all x1, waiting for transfers between devices, local(): lax.all_to_all(outgoing, ('gx', 'gy'), split_axis=0, concat_axis=3, tiled...  31.8 us
    all_to_all x1, starting transfers between devices, local(): lax.all_to_all(outgoing, ('gx', 'gy'), split_axis=0, concat_axis=3, tiled...  7.1 us
  transfers between devices with their start and end apart: 1, of which 1 were waited for; matrix products, arithmetic and copies ran while one was open for 0% of the time, Pallas kernels for 0%

profile of v5, /device:TPU:1, one launch (start us, length us, event | category | flops | bytes accessed | tf_op | source)
XLA Modules:
  0.0 319.5 jit_solution(2027704776504552184)
XLA Ops:
  0.0 0.7 broadcast_compare_fusion
  0.7 0.8 select_reduce_fusion
  1.5 0.1 convert_reduce_fusion
  1.6 3.1 copy.20
  4.7 0.7 fusion.4
  5.4 1.4 pack.1
  6.9 0.0 copy-start
  6.9 1.7 copy-done
  8.5 4.4 %copy.21 = bf16[32,3,128,64]{2,3,1,0:T(8,128)(2,1)} copy(bf16[32,3,128,64]{3,2,1,0:T(8,128)(2,1)} %copy-done) | data formatting | bytes 3145728 | tf_op jit(solution)/shard_map/pack/pallas_call | solution.py:27
  12.9 7.1 %all-to-all-start = ((bf16[32,3,128,64]{2,3,1,0:T(8,128)(2,1)}), bf16[32,3,128,64]{2,3,1,0:T(8,128)(2,1)S(1)}, u32[]{:S(2)}, u32[]{:S(2)}) async-start(bf16[32,3,128,64]{2,3,1,0:T(8,128)(2,1)} %copy.21), calls=%async_computation | async-start | bytes 3145728 | tf_op jit(solution)/shard_map/all_to_all | solution.py:349
  25.3 31.8 %all-to-all-done = bf16[32,3,128,64]{2,3,1,0:T(8,128)(2,1)S(1)} async-done(((bf16[32,3,128,64]{2,3,1,0:T(8,128)(2,1)}), bf16[32,3,128,64]{2,3,1,0:T(8,128)(2,1)S(1)}, u32[]{:S(2)}, u32[]{:S(2)}) %all-to-all-start) | async-done | bytes 1572896 | tf_op jit(solution)/shard_map/all_to_all | solution.py:349
  57.1 0.1 copy.22
  57.2 0.0 copy-start.1
  57.3 0.6 fusion
  57.8 0.7 copy.23
  58.5 0.0 copy-done.1
  58.6 260.9 %conditional.1 = (f32[1,1,12,128,512]{4,3,2,1,0:T(8,128)}) conditional(s32[]{:T(128)} %clamp.3, (s32[]{:T(128)}, bf16[12,128,512]{2,1,0:T(8,128)(2,1)S(1)}, s32[12,24]{1,0:T(8,128)S(1)}, f32[4]{0:T(128)S(1)}, bf16[12,24,128,128]{3,2,1,0:T(8,128)(2,1)}) %tuple.47, (s32[]{:T(128)}, bf16[12,128,512]{2,1,0:T(8,128)(2,1)S(1)}, ...), branch_computations={%region_6.7_spmd, %region_7.8_spmd, %region_8.9_spmd, %region_9.10... | conditional | flops 57 | bytes 559 | solution.py:392
  62.5 1.3 pad_add_fusion.1.meta_ref
  63.7 68.8 %halo_part.9 = (bf16[9,7,128,512]{3,2,1,0:T(8,128)(2,1)}, bf16[1,3,5,128,512]{4,3,2,1,0:T(8,128)(2,1)}) custom-call(s32[1]{0:T(128)} %bitcast.10.heavy_ref, bf16[12,128,512]{2,1,0:T(8,128)(2,1)S(1)} %get-tuple-element.111.panels_ref.refs_0_.refs_4_), custom_call_target="tpu_custom_call" | custom-call | tf_op jit(solution)/shard_map/cond/branch_3_fun/halo_part/pallas_call | solution.py:318
  132.5 16.7 %step1.7 = (bf16[12,128,512]{2,1,0:T(8,128)(2,1)}, f32[12,128,512]{2,1,0:T(8,128)}) custom-call(s32[2]{0:T(128)} %pad_add_fusion.1.meta_ref, s32[12,24]{1,0:T(8,128)S(1)} %get-tuple-element.109.pattern_ref, f32[4]{0:T(128)S(1)} %get-tuple-element.110.coeffs_ref, bf16[12,128,512]{2,1,0:T(8,128)(2,1)S(1)} %get-tuple-element.111.panels_ref.refs_0_.refs_4_, ...), custom_call_target="tpu_custom_call" | custom-call | tf_op jit(solution)/shard_map/cond/branch_3_fun/step1/pallas_call | solution.py:129
  149.3 67.4 %halo_part.10 = (bf16[9,7,128,512]{3,2,1,0:T(8,128)(2,1)}, bf16[1,3,5,128,512]{4,3,2,1,0:T(8,128)(2,1)}) custom-call(s32[1]{0:T(128)} %bitcast.10.heavy_ref, bf16[12,128,512]{2,1,0:T(8,128)(2,1)} %get-tuple-element.115.panels_ref.refs_0_), custom_call_target="tpu_custom_call" | custom-call | tf_op jit(solution)/shard_map/cond/branch_3_fun/halo_part/pallas_call | solution.py:318
  216.7 17.3 %step2.7 = (bf16[12,128,512]{2,1,0:T(8,128)(2,1)}, f32[12,128,512]{2,1,0:T(8,128)}) custom-call(s32[2]{0:T(128)} %pad_add_fusion.1.meta_ref, s32[12,24]{1,0:T(8,128)S(1)} %get-tuple-element.109.pattern_ref, f32[4]{0:T(128)S(1)} %get-tuple-element.110.coeffs_ref, bf16[12,128,512]{2,1,0:T(8,128)(2,1)} %get-tuple-element.115.panels_ref.refs_0_, ...), custom_call_target="tpu_custom_call" | custom-call | tf_op jit(solution)/shard_map/cond/branch_3_fun/step2/pallas_call | solution.py:129
  234.0 67.4 %halo_part.11 = (bf16[9,7,128,512]{3,2,1,0:T(8,128)(2,1)}, bf16[1,3,5,128,512]{4,3,2,1,0:T(8,128)(2,1)}) custom-call(s32[1]{0:T(128)} %bitcast.10.heavy_ref, bf16[12,128,512]{2,1,0:T(8,128)(2,1)} %get-tuple-element.118.panels_ref.refs_0_), custom_call_target="tpu_custom_call" | custom-call | tf_op jit(solution)/shard_map/cond/branch_3_fun/halo_part/pallas_call | solution.py:318
  301.4 18.1 %step3.7 = f32[12,128,512]{2,1,0:T(8,128)} custom-call(s32[2]{0:T(128)} %pad_add_fusion.1.meta_ref, s32[12,24]{1,0:T(8,128)S(1)} %get-tuple-element.109.pattern_ref, f32[4]{0:T(128)S(1)} %get-tuple-element.110.coeffs_ref, bf16[12,128,512]{2,1,0:T(8,128)(2,1)} %get-tuple-element.118.panels_ref.refs_0_, bf16[9,7,128,512]{3,2,1,0:T(8,128)(2,1)} %get-tuple-element.119.refs_1_, ...), custom_call_target="tpu_custom_call" | custom-call | tf_op jit(solution)/shard_map/cond/branch_3_fun/step3/pallas_call | solution.py:129
  (5 shorter events, 0.0 us)
Async XLA Ops:
  0.0 4.7 %copy-start.3 = (s32[32]{0:T(128)S(1)}, s32[32]{0:T(128)}, u32[]{:S(2)}) copy-start(s32[32]{0:T(128)} %param.9) | copy-start | bytes 388
  6.9 1.7 copy-start
  8.5 16.8 %copy-start.2 = (s32[1,1,12,24]{3,1,2,0:T(1,128)S(1)}, s32[1,1,12,24]{3,1,2,0:T(1,128)}, u32[]{:S(2)}) copy-start(s32[1,1,12,24]{3,1,2,0:T(1,128)} %param.12) | copy-start | bytes 3460
  12.9 44.2 %all-to-all-start = ((bf16[32,3,128,64]{2,3,1,0:T(8,128)(2,1)}), bf16[32,3,128,64]{2,3,1,0:T(8,128)(2,1)S(1)}, u32[]{:S(2)}, u32[]{:S(2)}) async-start(bf16[32,3,128,64]{2,3,1,0:T(8,128)(2,1)} %copy.21), calls=%async_computation | async-start | bytes 3145728 | tf_op jit(solution)/shard_map/all_to_all | solution.py:349
  57.2 1.3 copy-start.1
